TPU v7x, 32 devices: a whole 2x2x4 slice. The times are simulated.
32 devices in a mesh: lon: 16 (over z, y, core), lat: 2 (over x).
Axes of the slice: x: 2, y: 2, z: 4, core: 2. Of those that a mesh axis runs over, the one named last changes fastest.
Arguments:
- target: float32 [3, 32, 16384], P(None, 'lat', 'lon'), may hold values from -6 to 6
- grad_x: float32 [2, 3, 32, 16384], P(None, None, 'lat', 'lon'), may hold values from -6 to 6
- grad_y: float32 [2, 3, 32, 16384], P(None, None, 'lat', 'lon'), may hold values from -6 to 6
- labels: int32 [32, 16384], P('lat', 'lon'), may hold values from 0 to 1
- sweeps: int32 [3], replicated, may hold values from 2 to 4
Outputs:
- stitched: float32 [3, 32, 16384], P(None, 'lat', 'lon')
All inputs are finite; a program needn't handle non-finite values.
Results may differ from a plain program's by a relative error of at most 0.0004.
Values sent between devices are 32-bit elements; how exact they have to be, the bound alone decides.
No kernel may reach another device: no remote copies, remote signals or barrier semaphores. Data moves between devices by JAX's collectives and lax.ppermute only.
A program may use at most 64 MiB of HBM per device.

v0:
```python
import functools

import jax
import jax.numpy as jnp
from jax import lax
from jax.experimental import pallas as pl
from jax.experimental.pallas import tpu as pltpu
from jax.sharding import PartitionSpec as P

SCREENING = 0.02
DAMPING = 0.8
LEAST_SWEEPS = 2
LANES = 128
HALF = LANES // 2
SUBLANES = 8
VMEM = pl.BlockSpec(memory_space=pltpu.VMEM)
HBM = pl.BlockSpec(memory_space=pltpu.HBM)
F32 = functools.partial(jax.ShapeDtypeStruct, dtype=jnp.float32)
SCRATCH = functools.partial(pltpu.VMEM, dtype=jnp.float32)


def in_hbm(array):
    return pltpu.with_memory_space_constraint(array, pltpu.HBM)


def diagonal(scale):
    return SCREENING + 4.0 * scale


def rows_of(value):
    return lax.broadcasted_iota(jnp.int32, value.shape, 0)


def lanes_of(tile):
    return lax.broadcasted_iota(jnp.int32, tile.shape, len(tile.shape) - 1)


def tiles(value):
    return [value[:, k * LANES:(k + 1) * LANES] for k in range(value.shape[1] // LANES)]


def row_before(value):
    return jnp.where(rows_of(value) == 0, 0.0, pltpu.roll(value, 1, 0))


def row_after(value):
    last = value.shape[0] - 1
    return jnp.where(rows_of(value) == last, 0.0, pltpu.roll(value, last, 0))


def norths(planes):
    return [row_before(planes[-1])] + list(planes[:-1])


def souths(planes):
    return list(planes[1:]) + [row_after(planes[0])]


def west_of(value):
    return pltpu.roll(value, 1, 1)


def east_of(value):
    return pltpu.roll(value, value.shape[1] - 1, 1)


def neighbours(planes, combine):
    cut = [tiles(plane) for plane in planes]
    count, wide = len(cut), len(cut[0])
    lane = lanes_of(cut[0][0])
    out = []
    for t in range(count):
        westward = [None] * wide
        eastward = [None] * wide

        def rolled(known, k, shift):
            k %= wide
            if known[k] is None:
                known[k] = pltpu.roll(cut[t][k], shift, 1)
            return known[k]

        done = []
        for k in range(wide):
            north = cut[t - 1][k] if t else row_before(cut[-1][k])
            south = cut[t + 1][k] if t + 1 < count else row_after(cut[0][k])
            west = jnp.where(lane == 0, rolled(westward, k - 1, 1), rolled(westward, k, 1))
            east = jnp.where(lane == LANES - 1, rolled(eastward, k + 1, LANES - 1), rolled(eastward, k, LANES - 1))
            done.append(combine(t, k, cut[t][k], (north + south) + (west + east)))
        out.append(jnp.concatenate(done, 1))
    return out


def sweep(planes, scaled, scale, inside=None):
    beside = DAMPING * scale / diagonal(scale)

    def combine(t, k, value, total):
        value = (1.0 - DAMPING) * value + (scaled(t, k) + beside * total)
        return value if inside is None else value * inside[t]

    return tuple(neighbours(planes, combine))


def residual(planes, right, scale):
    return neighbours(planes, lambda t, k, value, total: right(t, k) - diagonal(scale) * value + scale * total)


def span(k):
    return slice(k * LANES, (k + 1) * LANES)


def repeat(step, sweeps, level, fields, written, ready=lambda: None):
    for i in range(written):
        fields = step(i, fields)
    ready()
    return lax.fori_loop(LEAST_SWEEPS, sweeps[level], step, fields)


def load_planes(ref, start, count, height):
    def plane(first):
        rows = pl.ds(first, height, stride=count) if count > 1 else pl.ds(first, height)
        return jnp.concatenate([ref[k, rows, :] for k in range(ref.shape[0])], 1)

    return [plane(start + t) for t in range(count)]


def store_planes(ref, start, planes):
    count, height = len(planes), planes[0].shape[0]
    for t, plane in enumerate(planes):
        rows = pl.ds(start + t, height, stride=count) if count > 1 else pl.ds(start + t, height)
        for k, tile in enumerate(tiles(plane)):
            ref[k, rows, :] = tile


def places_of(shape, wanted):
    source = lax.broadcasted_iota(jnp.int32, shape, 0)
    target = lax.broadcasted_iota(jnp.int32, shape, 1)
    return wanted(source, target).astype(jnp.float32).astype(jnp.bfloat16)


def halo_coarse(fine):
    return jnp.where(fine < HALF, fine // 2, HALF + fine // 2)


def pairing():
    own = places_of((2 * LANES, LANES), lambda source, target: source // 2 == target)
    halo = places_of((LANES, LANES), lambda source, target: halo_coarse(source) == target)
    return own, halo


def spreading():
    own = places_of((2 * LANES, 2 * LANES), lambda source, target: source == target // 2 + LANES * (target % 2))
    halo = places_of((2 * LANES, LANES), lambda source, target: source == halo_coarse(target) + LANES * (target % 2))
    return own, halo


def moved(value, places):
    high = value.astype(jnp.bfloat16)
    low = (value - high.astype(jnp.float32)).astype(jnp.bfloat16)
    dot = functools.partial(jnp.dot, preferred_element_type=jnp.float32)
    return dot(high, places) + dot(low, places)


def moved_blocks(own_blocks, halo_blocks, places):
    rows, count = halo_blocks[0].shape[0], len(own_blocks[0])
    packed = moved(jnp.concatenate([block for blocks in own_blocks for block in blocks], 0), places[0])
    edges = moved(jnp.concatenate(halo_blocks, 0), places[1])
    out = []
    for i in range(len(own_blocks)):
        parts = [packed[(i * count + k) * rows:(i * count + k + 1) * rows] for k in range(count)]
        out.append(jnp.concatenate(parts + [edges[i * rows:(i + 1) * rows]], 1))
    return out


def pair_columns(fields, places):
    cols = fields[0].shape[1] - LANES
    width = 2 * LANES
    own = [[f[:, k * width:(k + 1) * width] for k in range(cols // width)] for f in fields]
    return moved_blocks(own, [f[:, cols:] for f in fields], places)


def spread_columns(fields, places):
    cut = [list(zip(tiles(0.75 * f + 0.25 * west_of(f)), tiles(0.75 * f + 0.25 * east_of(f)))) for f in fields]
    blocks = [[jnp.concatenate(both, 1) for both in field] for field in cut]
    return moved_blocks([b[:-1] for b in blocks], [b[-1] for b in blocks], places)


def prolong(fields, places):
    halves = [
        half
        for planes in fields
        for value, north, south in zip(planes, norths(planes), souths(planes))
        for half in (0.75 * value + 0.25 * north, 0.75 * value + 0.25 * south)
    ]
    spread = spread_columns(halves, places)
    count = 2 * len(fields[0])
    return [spread[i * count:(i + 1) * count] for i in range(len(fields))]


def window_of(rows, parts):
    return rows + (2 * SUBLANES if parts > 2 else SUBLANES if parts == 2 else 0)


def own_start(parts, place):
    return 0 if parts == 1 else pl.multiple_of(SUBLANES * place, SUBLANES) if parts == 2 else SUBLANES


def band_masks(window, parts, place, rows):
    if parts <= 2:
        return None
    count = window // SUBLANES
    first = place * rows - SUBLANES
    row = [first + t + count * lax.broadcasted_iota(jnp.int32, (SUBLANES, 1), 0) for t in range(count)]
    return [((r >= 0) & (r < parts * rows)).astype(jnp.float32) for r in row]


def eastward(own_last, halo):
    return jnp.where(lanes_of(halo) < HALF, halo, own_last)


def westward(own_first, halo):
    return jnp.where(lanes_of(halo) < HALF, own_first, halo)


def with_edges(parts, from_west, from_east):
    inner = lanes_of(from_west) < HALF
    first = parts[0] + jnp.where(inner, from_west, 0.0)
    last = parts[-2] + jnp.where(inner, 0.0, from_east)
    halo = parts[-1] + jnp.where(inner, from_east, from_west)
    return [first] + list(parts[1:-2]) + [last, halo]


COARSE_WIDTH, FINE_WIDTH, REACH = 32, 8, 4
TO_EAST, TO_WEST = -24, -8


def in_window(lane, start, width):
    start = start % LANES
    end = start + width
    return (lane >= start) & (lane < end) if end <= LANES else (lane >= start) | (lane < end - LANES)


def slots(value_rows, right_rows, coarse_rows, coarse_start):
    out, at = [], 0
    for which, rows, start, width in (
        (2, coarse_rows, coarse_start, COARSE_WIDTH),
        (0, value_rows, -REACH, FINE_WIDTH),
        (1, right_rows, -REACH, FINE_WIDTH),
    ):
        for first in range(0, rows, SUBLANES):
            out.append((which, first, min(SUBLANES, rows - first), start, width, at))
            at += width
    assert at <= LANES
    return out


def bundle(fields, coarse_start):
    out = jnp.zeros((SUBLANES, LANES), jnp.float32)
    lane = lanes_of(out)
    for which, first, rows, start, width, at in slots(*(f.shape[0] for f in fields), coarse_start):
        piece = fields[which][first:first + rows]
        if rows < SUBLANES:
            piece = jnp.concatenate([piece, jnp.zeros((SUBLANES - rows, LANES), jnp.float32)], 0)
        out = jnp.where(in_window(lane, at, width), pltpu.roll(piece, (at - start) % LANES, 1), out)
    return out


def unbundle(tile, heights, coarse_start):
    lane = lanes_of(tile)
    pieces = ([], [], [])
    for which, first, rows, start, width, at in slots(*heights, coarse_start):
        piece = jnp.where(in_window(lane, start, width), pltpu.roll(tile, (start - at) % LANES, 1), 0.0)
        pieces[which].append(piece[:rows])
    return [jnp.concatenate(p, 0) if len(p) > 1 else p[0] for p in pieces]


VALUE_ROWS, RIGHT_ROWS, COARSE_ROWS = 8, 4, 12
ACROSS = (VALUE_ROWS, RIGHT_ROWS, COARSE_ROWS)


def pack(value, right, coarse):
    halves = right[:-1] + [c[SUBLANES:] for c in coarse[:-1]]
    joined = [jnp.concatenate(halves[k:k + 2], 0) for k in range(0, len(halves), 2)]
    return value[:-1] + [c[:SUBLANES] for c in coarse[:-1]] + joined + [bundle([value[-1], right[-1], coarse[-1]], TO_WEST)]


def packed_tiles(fine, coarse):
    return fine + coarse + (fine + coarse) // 2 + 1


def unpack(tile, fine, coarse):
    halves = []
    for k in range(fine + coarse, fine + coarse + (fine + coarse) // 2):
        both = tile(k)
        halves += [both[:4], both[4:]]
    value = [tile(k) for k in range(fine)]
    right = halves[:fine]
    low = [jnp.concatenate([tile(fine + k), halves[fine + k]], 0) for k in range(coarse)]
    ends = unbundle(tile(packed_tiles(fine, coarse) - 1), ACROSS, TO_WEST)
    return [field + [end] for field, end in zip((value, right, low), ends)]


def down_kernel(parts, sweeps_hbm, target, grad_x, grad_y, labels, *refs):
    sent = 5 if parts == 2 else 0
    value_ref, right_ref, coarse_ref = refs[:3]
    sent_refs = refs[3:3 + sent]
    sweeps, target_v, grad_x_v, grad_y_v, labels_v, v_ref, b_ref, scaled_ref, resid_ref, sems = refs[3 + sent:]
    chans, rows, cols = target.shape
    window = value_ref.shape[2]
    count = window // SUBLANES
    place = lax.axis_index("lat")
    start = own_start(parts, place)
    inside = band_masks(window, parts, place, rows)
    scale = 1.0

    first_copies = [
        pltpu.make_async_copy(labels, labels_v, sems.at[chans, 0]),
        pltpu.make_async_copy(sweeps_hbm, sweeps, sems.at[chans, 1]),
    ]
    for copy in first_copies:
        copy.start()
    copies = []
    for chan in range(chans):
        copies.append([
            pltpu.make_async_copy(target.at[chan], target_v.at[chan], sems.at[chan, 0]),
            pltpu.make_async_copy(grad_x.at[:, chan], grad_x_v.at[:, chan], sems.at[chan, 1]),
            pltpu.make_async_copy(grad_y.at[:, chan], grad_y_v.at[:, chan], sems.at[chan, 2]),
        ])
        for copy in copies[-1]:
            copy.start()
    if window > rows:
        v_ref[...] = jnp.zeros_like(v_ref)
        b_ref[...] = jnp.zeros_like(b_ref)
    places = pairing()
    for copy in first_copies:
        copy.wait()

    def chosen(grad, chan):
        marks = labels_v[...]
        out = jnp.zeros((rows, cols), jnp.float32)
        for source in range(grad.shape[0]):
            out = jnp.where(marks == source, grad[source, chan], out)
        return out

    blank = jnp.zeros((rows, LANES), jnp.float32)
    fields = []
    for chan in range(chans):
        for copy in copies[chan]:
            copy.wait()
        own = jnp.concatenate([target_v[chan], blank], 1)
        sel_x = jnp.concatenate([chosen(grad_x_v, chan), blank], 1)
        sel_y = jnp.concatenate([chosen(grad_y_v, chan), blank], 1)
        right = SCREENING * own - ((sel_x - west_of(sel_x)) + (sel_y - row_before(sel_y)))
        below = pltpu.roll(sel_y[rows - SUBLANES:], 1, 0)
        below = jnp.where(rows_of(below) == 0, below, 0.0)
        for k, (v, b, s) in enumerate(zip(tiles(own), tiles(right), tiles(below))):
            v_ref[chan, k, pl.ds(start, rows), :] = v
            b_ref[chan, k, pl.ds(start, rows), :] = b
            if window > rows:
                b_ref[chan, k, pl.ds(start + rows, SUBLANES), :] = s
    for chan in range(chans):
        fields.append(tuple(load_planes(v_ref.at[chan], 0, count, SUBLANES)))
        right = load_planes(b_ref.at[chan], 0, count, SUBLANES)
        if inside is not None:
            right = [b * mask for b, mask in zip(right, inside)]
        store_planes(right_ref.at[chan], 0, right)
        for t in range(count):
            scaled_ref[chan, t] = (DAMPING / diagonal(scale)) * right[t]

    def step(_, fields):
        return tuple(
            sweep(planes, lambda t, k, chan=chan: scaled_ref[chan, t, :, span(k)], scale, inside)
            for chan, planes in enumerate(fields)
        )

    fields = repeat(step, sweeps, 0, tuple(fields), LEAST_SWEEPS)
    paired = []
    for chan, planes in enumerate(fields):
        store_planes(value_ref.at[chan], 0, planes)
        back = diagonal(scale) / DAMPING
        left = residual(planes, lambda t, k, chan=chan: back * scaled_ref[chan, t, :, span(k)], scale)
        if inside is not None:
            left = [r * mask for r, mask in zip(left, inside)]
        store_planes(resid_ref.at[chan], 0, left)
    for chan in range(chans):
        north, south = load_planes(resid_ref.at[chan], 0, 2, window // 2)
        paired.append(north + south)
    coarse = pair_columns(paired, places)
    for chan in range(chans):
        low = 0.25 * coarse[chan]
        coarse_ref[chan] = low
        if parts != 2:
            continue
        packed_ref, east_across, east_ref, west_across, west_ref = sent_refs
        wide = value_ref.shape[1]
        value = [value_ref[chan, k] for k in range(wide)]
        right = [right_ref[chan, k] for k in range(wide)]
        low = tiles(low)
        north = place == 0
        value_border = [jnp.where(north, v[12:20], v[4:12]) for v in value]
        right_border = [jnp.where(north, b[13:17], b[8:12]) for b in right]
        for k, tile in enumerate(pack(value_border, right_border, low)):
            packed_ref[chan, k] = tile
        for east, west, fields in (
            (east_ref, west_ref, (value, right, low)),
            (east_across, west_across, (value_border, right_border, low)),
        ):
            east[chan] = bundle([eastward(f[-2], f[-1]) for f in fields], TO_EAST)
            west[chan] = bundle([westward(f[0], f[-1]) for f in fields], TO_WEST)


def down(parts, sweeps, target, grad_x, grad_y, labels):
    chans, rows, cols = target.shape
    window = window_of(rows, parts)
    wide, half = cols // LANES + 1, cols // 2 // LANES + 1
    spare = SUBLANES if window > rows else 0
    outs = [F32((chans, wide, window, LANES))] * 2 + [F32((chans, window // 2, half * LANES))]
    if parts == 2:
        outs.append(F32((chans, packed_tiles(wide - 1, half - 1), SUBLANES, LANES)))
        outs += [F32((chans, SUBLANES, LANES))] * 4
    return pl.pallas_call(
        functools.partial(down_kernel, parts),
        in_specs=[HBM] * 5,
        out_specs=[VMEM] * len(outs),
        out_shape=outs,
        scratch_shapes=[
            pltpu.SMEM(sweeps.shape, jnp.int32),
            SCRATCH(target.shape),
            SCRATCH(grad_x.shape),
            SCRATCH(grad_y.shape),
            pltpu.VMEM(labels.shape, jnp.int32),
            SCRATCH((chans, wide, window + spare, LANES)),
            SCRATCH((chans, wide, window + spare, LANES)),
            SCRATCH((chans, window // SUBLANES, SUBLANES, wide * LANES)),
            SCRATCH((chans, wide, window, LANES)),
            pltpu.SemaphoreType.DMA((chans + 1, 3)),
        ],
        compiler_params=pltpu.CompilerParams(vmem_limit_bytes=32 * 2**20),
        name="down",
    )(*(in_hbm(a) for a in (sweeps, target, grad_x, grad_y, labels)))


def joined(place, own, other, height):
    gap = jnp.zeros((height - own.shape[0], own.shape[1]), jnp.float32)
    top, bottom = (lambda v: jnp.concatenate([v, gap], 0)), (lambda v: jnp.concatenate([gap, v], 0))
    return jnp.where(place == 0, top(own) + bottom(other), bottom(own) + top(other))


def up_kernel(parts, sweeps_hbm, value_ref, right_ref, coarse_ref, *refs):
    received = 5 if parts == 2 else 0
    packed_ref, *edge_refs = refs[:received] or [None]
    out_hbm, sweeps, v0_ref, b0_ref, k0_ref, b1_ref, k1_ref, k2_ref, fix_ref, out_ref, sems = refs[received:]
    sweeps_copy = pltpu.make_async_copy(sweeps_hbm, sweeps, sems.at[0])
    sweeps_copy.start()
    chans, rows, cols = out_ref.shape
    wide, window = value_ref.shape[1:3]
    half = coarse_ref.shape[2] // LANES
    full = parts * rows
    count0, count1, count2 = window // SUBLANES, max(1, full // 2 // SUBLANES), max(1, full // 4 // SUBLANES)
    place = lax.axis_index("lat")
    inside = band_masks(window, parts, place, rows)
    own_heights = (window, window, window // 2)

    def sides(chan, across):
        heights = ACROSS if across else own_heights
        from_west = unbundle(edge_refs[1 - across][chan], heights, TO_EAST)
        from_east = unbundle(edge_refs[3 - across][chan], heights, TO_WEST)
        return list(zip(from_west, from_east))

    from_partner = []
    for chan in range(chans):
        low = coarse_ref[chan]
        if parts == 2:
            here, there = sides(chan, 0), sides(chan, 1)
            other = unpack(lambda k: packed_ref[chan, k], wide - 1, half - 1)
            value, right, other_low = (with_edges(f, *s) for f, s in zip(other, there))
            low = jnp.concatenate(with_edges(tiles(low), *here[2]), 1)
            low = joined(place, low, jnp.concatenate(other_low, 1), full // 2)
            for ref, own, side in ((v0_ref, value_ref, here[0]), (b0_ref, right_ref, here[1])):
                for k, tile in enumerate(with_edges([own[chan, k] for k in range(wide)], *side)):
                    ref[chan, k] = tile
            from_partner.append((value, right))
        else:
            v0_ref[chan] = value_ref[chan]
            b0_ref[chan] = right_ref[chan]
        for k, tile in enumerate(tiles(low)):
            b1_ref[chan, k] = tile

    def add_rows(value_at, right_at):
        for chan, (value, right) in enumerate(from_partner):
            for k in range(wide):
                v0_ref[chan, k, pl.ds(value_at, VALUE_ROWS), :] += value[k]
                b0_ref[chan, k, pl.ds(right_at, RIGHT_ROWS), :] += right[k]

    if parts == 2:
        pl.when(place == 0)(lambda: add_rows(12, 16))
        pl.when(place == 1)(lambda: add_rows(4, 5))

    def smoothed(fields, scaled_ref, level, written=LEAST_SWEEPS, ready=lambda: None):
        def step(_, fields):
            return tuple(
                sweep(planes, lambda t, k, i=i: scaled_ref[i, t, :, span(k)], 0.25**level)
                for i, planes in enumerate(fields)
            )

        return repeat(step, sweeps, level, tuple(tuple(f) for f in fields), written, ready)

    def from_zero(rights, scaled_ref, level, ready=lambda: None):
        first = [[(DAMPING / diagonal(0.25**level)) * b for b in planes] for planes in rights]
        for i, planes in enumerate(first):
            for t, plane in enumerate(planes):
                scaled_ref[i, t] = plane
        return smoothed(first, scaled_ref, level, LEAST_SWEEPS - 1, ready)

    pair_places, spread_places = pairing(), spreading()
    height1 = full // 2 // count1
    right1 = [load_planes(b1_ref.at[i], 0, count1, height1) for i in range(chans)]
    mid = from_zero(right1, k1_ref, 1, sweeps_copy.wait)
    back = diagonal(0.25) / DAMPING
    left = [residual(f, lambda t, k, i=i: back * k1_ref[i, t, :, span(k)], 0.25) for i, f in enumerate(mid)]
    pairs = [f[t] + f[t + 1] for f in left for t in range(0, count1, 2)]
    low = [0.25 * v for v in pair_columns(pairs, pair_places)]
    right2 = [low[i * count2:(i + 1) * count2] for i in range(chans)]
    fix2 = from_zero(right2, k2_ref, 2)
    mid = [[v + f for v, f in zip(planes, fix)] for planes, fix in zip(mid, prolong(fix2, spread_places))]
    mid = smoothed(mid, k1_ref, 1)
    spare = (fix_ref.shape[2] - full) // 2
    if spare:
        fix_ref[...] = jnp.zeros_like(fix_ref)
    for i, fix in enumerate(prolong(mid, spread_places)):
        store_planes(fix_ref.at[i], spare, fix)
    shown = pl.multiple_of((SUBLANES if parts == 2 else rows) * place, SUBLANES)
    start = own_start(parts, place)
    fields = []
    for i in range(chans):
        planes = load_planes(v0_ref.at[i], 0, count0, SUBLANES)
        fix = load_planes(fix_ref.at[i], shown, count0, SUBLANES)
        fields.append(tuple(v + f for v, f in zip(planes, fix)))
        for t, b in enumerate(load_planes(b0_ref.at[i], 0, count0, SUBLANES)):
            k0_ref[i, t] = (DAMPING / diagonal(1.0)) * b

    def step(_, fields):
        return tuple(
            sweep(planes, lambda t, k, i=i: k0_ref[i, t, :, span(k)], 1.0, inside) for i, planes in enumerate(fields)
        )

    fields = repeat(step, sweeps, 0, tuple(fields), LEAST_SWEEPS)
    out_copies = []
    for i, planes in enumerate(fields):
        store_planes(v0_ref.at[i], 0, planes)
        for k in range(cols // LANES):
            out_ref[i, :, k * LANES:(k + 1) * LANES] = v0_ref[i, k, pl.ds(start, rows), :]
        out_copies.append(pltpu.make_async_copy(out_ref.at[i], out_hbm.at[i], sems.at[1 + i]))
        out_copies[-1].start()
    for copy in out_copies:
        copy.wait()


def up(parts, shape, sweeps, value, right, coarse, *received):
    chans, rows, cols = shape
    wide, window = value.shape[1:3]
    full = parts * rows
    half, quarter = cols // 2 // LANES + 1, cols // 4 // LANES + 1
    count1, count2 = max(1, full // 2 // SUBLANES), max(1, full // 4 // SUBLANES)
    spare = 2 * SUBLANES if parts > 2 else 0
    return pl.pallas_call(
        functools.partial(up_kernel, parts),
        in_specs=[HBM] + [VMEM] * (3 + len(received)),
        out_specs=HBM,
        out_shape=F32(shape),
        scratch_shapes=[
            pltpu.SMEM(sweeps.shape, jnp.int32),
            SCRATCH(value.shape),
            SCRATCH(value.shape),
            SCRATCH((chans, window // SUBLANES, SUBLANES, wide * LANES)),
            SCRATCH((chans, half, full // 2, LANES)),
            SCRATCH((chans, count1, full // 2 // count1, half * LANES)),
            SCRATCH((chans, count2, full // 4 // count2, quarter * LANES)),
            SCRATCH((chans, wide, full + spare, LANES)),
            SCRATCH(shape),
            pltpu.SemaphoreType.DMA((1 + chans,)),
        ],
        compiler_params=pltpu.CompilerParams(vmem_limit_bytes=48 * 2**20),
        name="up",
    )(in_hbm(sweeps), value, right, coarse, *received)


def local(target, grad_x, grad_y, labels, sweeps):
    parts, around_globe = lax.axis_size("lat"), lax.axis_size("lon")
    value, right, coarse, *sent = down(parts, sweeps, target, grad_x, grad_y, labels)
    eastward_pairs = [(i, (i + 1) % around_globe) for i in range(around_globe)]
    westward_pairs = [(j, i) for i, j in eastward_pairs]
    if parts < 2:
        raise NotImplementedError
    if parts == 2:
        def across(pairs):
            return [(2 * i + k, 2 * j + 1 - k) for i, j in pairs for k in range(2)]

        packed, east_across, east, west_across, west = sent
        packed = lax.ppermute(packed, "lat", [(0, 1), (1, 0)])
        across_west = lax.ppermute(east_across, ("lon", "lat"), across(eastward_pairs))
        from_west = lax.ppermute(east, "lon", eastward_pairs)
        across_east = lax.ppermute(west_across, ("lon", "lat"), across(westward_pairs))
        from_east = lax.ppermute(west, "lon", westward_pairs)
        received = (packed, across_west, from_west, across_east, from_east)
        return up(parts, target.shape, sweeps, value, right, coarse, *received)

    chans, half_rows = coarse.shape[:2]
    coarse = coarse.reshape(chans, half_rows, -1, LANES).transpose(0, 2, 1, 3)

    def shared_lon(field):
        parts_of = [field[:, k] for k in range(field.shape[1])]
        from_west = lax.ppermute(eastward(parts_of[-2], parts_of[-1]), "lon", eastward_pairs)
        from_east = lax.ppermute(westward(parts_of[0], parts_of[-1]), "lon", westward_pairs)
        return jnp.stack(with_edges(parts_of, from_west, from_east), 1)

    value, right, coarse = (shared_lon(f) for f in (value, right, coarse))
    if parts > 2:
        rows = target.shape[1]
        spare = 2 * SUBLANES
        southward = [(i, i + 1) for i in range(parts - 1)]
        northward = [(i + 1, i) for i in range(parts - 1)]

        def shared_lat(field):
            north = lax.ppermute(field[:, :, rows:], "lat", southward)
            south = lax.ppermute(field[:, :, :spare], "lat", northward)
            zeros = jnp.zeros_like(south)
            return field + jnp.concatenate([north, zeros], 2) + jnp.concatenate([zeros, south], 2)

        value, right = shared_lat(value), shared_lat(right)
        every = lax.all_gather(coarse, "lat")
        step = rows // 2
        total = jnp.zeros((chans, coarse.shape[1], parts * step + SUBLANES, LANES), jnp.float32)
        for i in range(parts):
            total = total.at[:, :, i * step:i * step + step + SUBLANES].add(every[i])
        coarse = total[:, :, 4:-4]
    coarse = coarse.transpose(0, 2, 1, 3).reshape(chans, coarse.shape[2], -1)
    return up(parts, target.shape, sweeps, value, right, coarse)


def solution(mesh):
    in_specs = (
        P(None, "lat", "lon"),
        P(None, None, "lat", "lon"),
        P(None, None, "lat", "lon"),
        P("lat", "lon"),
        P(),
    )
    out_specs = P(None, "lat", "lon")
    return jax.shard_map(local, mesh=mesh, in_specs=in_specs, out_specs=out_specs, check_vma=False)
```

profile of v0, /device:TPU:0, one launch (start us, length us, event | category | flops | bytes accessed | tf_op | source)
XLA Modules:
  0.0 16.7 jit_solution(8044081614489933101)
XLA Ops:
  0.0 2.7 %down.1 = (f32[3,9,24,128]{3,2,1,0:T(8,128)S(1)}, f32[3,9,24,128]{3,2,1,0:T(8,128)S(1)}, f32[3,12,640]{2,1,0:T(8,128)S(1)}, f32[3,19,8,128]{3,2,1,0:T(8,128)S(1)...) custom-call(s32[3]{0:T(128)} %sweeps_hbm.3, ...), custom_call_target="tpu_custom_call" | custom-call | tf_op jit(solution)/shard_map/down/pallas_call | solution.py:420
  2.7 3.0 %collective-permute-start = (f32[3,19,8,128]{3,2,1,0:T(8,128)S(1)}, f32[3,19,8,128]{3,2,1,0:T(8,128)S(1)}, u32[]{:S(2)}, u32[]{:S(2)}) collective-permute-start(f32[3,19,8,128]{3,2,1,0:T(8,128)S(1)} %get-tuple-element.16), channel_id=1, source_target_pairs={{0,1},{1,0},{2,3},{3,2},{4,5},{5,4},{6,7},{7,6},{8,9},{9,8},{10,11... | collective-permute-start | bytes 700424 | tf_op jit(solution)/shard_map/ppermute | solution.py:599
  5.7 0.0 collective-permute-start.1
  5.7 1.6 %collective-permute-start.2 = (f32[3,8,128]{2,1,0:T(8,128)S(1)}, f32[3,8,128]{2,1,0:T(8,128)S(1)}, u32[]{:S(2)}, u32[]{:S(2)}) collective-permute-start(f32[3,8,128]{2,1,0:T(8,128)S(1)} %get-tuple-element.18), channel_id=1, source_target_pairs={{0,2},{2,4},{4,6},{6,8},{8,10},{10,12},{12,14},{14,16},{16,18},{18... | collective-permute-start | bytes 36872 | tf_op jit(solution)/shard_map/ppermute | solution.py:601
  7.3 3.7 %collective-permute-start.3 = (f32[3,8,128]{2,1,0:T(8,128)S(1)}, f32[3,8,128]{2,1,0:T(8,128)S(1)}, u32[]{:S(2)}, u32[]{:S(2)}) collective-permute-start(f32[3,8,128]{2,1,0:T(8,128)S(1)} %get-tuple-element.19), channel_id=1, source_target_pairs={{2,1},{3,0},{4,3},{5,2},{6,5},{7,4},{8,7},{9,6},{10,9},{11,8},{12,... | collective-permute-start | bytes 36872 | tf_op jit(solution)/shard_map/ppermute | solution.py:602
  11.1 0.7 %collective-permute-start.4 = (f32[3,8,128]{2,1,0:T(8,128)S(1)}, f32[3,8,128]{2,1,0:T(8,128)S(1)}, u32[]{:S(2)}, u32[]{:S(2)}) collective-permute-start(f32[3,8,128]{2,1,0:T(8,128)S(1)} %get-tuple-element.20), channel_id=1, source_target_pairs={{2,0},{4,2},{6,4},{8,6},{10,8},{12,10},{14,12},{16,14},{18,16},{20... | collective-permute-start | bytes 36872 | tf_op jit(solution)/shard_map/ppermute | solution.py:603
  11.7 0.8 %collective-permute-done.1.refs_1_ = f32[3,8,128]{2,1,0:T(8,128)S(1)} collective-permute-done((f32[3,8,128]{2,1,0:T(8,128)S(1)}, f32[3,8,128]{2,1,0:T(8,128)S(1)}, u32[]{:S(2)}, u32[]{:S(2)}) %collective-permute-start.1) | collective-permute-done | bytes 12320 | tf_op jit(solution)/shard_map/ppermute | solution.py:600
  12.5 0.0 collective-permute-done.2.refs_2_
  12.5 0.0 collective-permute-done.3.refs_3_
  12.5 0.6 %collective-permute-done.4.refs_4_ = f32[3,8,128]{2,1,0:T(8,128)S(1)} collective-permute-done((f32[3,8,128]{2,1,0:T(8,128)S(1)}, f32[3,8,128]{2,1,0:T(8,128)S(1)}, u32[]{:S(2)}, u32[]{:S(2)}) %collective-permute-start.4) | collective-permute-done | bytes 12320 | tf_op jit(solution)/shard_map/ppermute | solution.py:603
  13.1 0.0 collective-permute-done.refs_0_
  13.1 3.5 %up.1 = f32[3,16,1024]{2,1,0:T(8,128)} custom-call(s32[3]{0:T(128)} %sweeps_hbm.3, f32[3,9,24,128]{3,2,1,0:T(8,128)S(1)} %get-tuple-element.13.value_ref, f32[3,9,24,128]{3,2,1,0:T(8,128)S(1)} %get-tuple-element.14.right_ref, f32[3,12,640]{2,1,0:T(8,128)S(1)} %get-tuple-element.15.coarse_ref, f32[3,19,8,128]{3,2,1,0:T(8,128)S(1)} %collective-permute-done.refs_0_, ...), custom_call_target="tpu_custom_call" | custom-call | tf_op jit(solution)/shard_map/up/pallas_call | solution.py:565
Async XLA Ops:
  2.7 10.4 %collective-permute-start = (f32[3,19,8,128]{3,2,1,0:T(8,128)S(1)}, f32[3,19,8,128]{3,2,1,0:T(8,128)S(1)}, u32[]{:S(2)}, u32[]{:S(2)}) collective-permute-start(f32[3,19,8,128]{3,2,1,0:T(8,128)S(1)} %get-tuple-element.16), channel_id=1, source_target_pairs={{0,1},{1,0},{2,3},{3,2},{4,5},{5,4},{6,7},{7,6},{8,9},{9,8},{10,11... | collective-permute-start | bytes 700424 | tf_op jit(solution)/shard_map/ppermute | solution.py:599
  5.7 6.8 %collective-permute-start.1 = (f32[3,8,128]{2,1,0:T(8,128)S(1)}, f32[3,8,128]{2,1,0:T(8,128)S(1)}, u32[]{:S(2)}, u32[]{:S(2)}) collective-permute-start(f32[3,8,128]{2,1,0:T(8,128)S(1)} %get-tuple-element.17), channel_id=1, source_target_pairs={{0,3},{1,2},{2,5},{3,4},{4,7},{5,6},{6,9},{7,8},{8,11},{9,10},{10,... | collective-permute-start | bytes 36872 | tf_op jit(solution)/shard_map/ppermute | solution.py:600
  5.7 6.8 %collective-permute-start.2 = (f32[3,8,128]{2,1,0:T(8,128)S(1)}, f32[3,8,128]{2,1,0:T(8,128)S(1)}, u32[]{:S(2)}, u32[]{:S(2)}) collective-permute-start(f32[3,8,128]{2,1,0:T(8,128)S(1)} %get-tuple-element.18), channel_id=1, source_target_pairs={{0,2},{2,4},{4,6},{6,8},{8,10},{10,12},{12,14},{14,16},{16,18},{18... | collective-permute-start | bytes 36872 | tf_op jit(solution)/shard_map/ppermute | solution.py:601
  7.3 5.2 %collective-permute-start.3 = (f32[3,8,128]{2,1,0:T(8,128)S(1)}, f32[3,8,128]{2,1,0:T(8,128)S(1)}, u32[]{:S(2)}, u32[]{:S(2)}) collective-permute-start(f32[3,8,128]{2,1,0:T(8,128)S(1)} %get-tuple-element.19), channel_id=1, source_target_pairs={{2,1},{3,0},{4,3},{5,2},{6,5},{7,4},{8,7},{9,6},{10,9},{11,8},{12,... | collective-permute-start | bytes 36872 | tf_op jit(solution)/shard_map/ppermute | solution.py:602
  11.1 2.1 %collective-permute-start.4 = (f32[3,8,128]{2,1,0:T(8,128)S(1)}, f32[3,8,128]{2,1,0:T(8,128)S(1)}, u32[]{:S(2)}, u32[]{:S(2)}) collective-permute-start(f32[3,8,128]{2,1,0:T(8,128)S(1)} %get-tuple-element.20), channel_id=1, source_target_pairs={{2,0},{4,2},{6,4},{8,6},{10,8},{12,10},{14,12},{16,14},{18,16},{20... | collective-permute-start | bytes 36872 | tf_op jit(solution)/shard_map/ppermute | solution.py:603
where the time goes:
time: 16.5 us; the launch traced here: 16.7 us
  starting transfers between devices  9.02 us (55%)
  Pallas kernels  6.24 us (38%)
  waiting for transfers between devices  1.41 us (9%)
    ppermute x1, starting transfers between devices, local(): lax.ppermute(west_across, ('lon', 'lat'), across(westward_pairs))  3.74 us
    pallas_call x1, Pallas kernels, up(): pl.pallas_call(functools.partial(up_kernel, parts), in_specs=[HBM] + [VME...  3.54 us
    ppermute x1, starting transfers between devices, local(): packed = lax.ppermute(packed, 'lat', [(0, 1), (1, 0)])  3 us
    pallas_call x1, Pallas kernels, down(): pl.pallas_call(functools.partial(down_kernel, parts), in_specs=[HBM] * 5,...  2.7 us
    ppermute x1, starting transfers between devices, local(): from_west = lax.ppermute(east, 'lon', eastward_pairs)  1.6 us
    ppermute x1, waiting for transfers between devices, local(): lax.ppermute(east_across, ('lon', 'lat'), across(eastward_pairs))  0.8 us
    ppermute x1, starting transfers between devices, local(): from_east = lax.ppermute(west, 'lon', westward_pairs)  0.68 us
    ppermute x1, waiting for transfers between devices, local(): from_east = lax.ppermute(west, 'lon', westward_pairs)  0.6 us
  transfers between devices with their start and end apart: 5, of which 2 were waited for; matrix products, arithmetic and copies ran while one was open for 0% of the time, Pallas kernels for 0%

commit v1 on v0

v1 whole, which is shorter than its diff:
```python
import functools

import jax
import jax.numpy as jnp
from jax import lax
from jax.experimental import pallas as pl
from jax.experimental.pallas import tpu as pltpu
from jax.sharding import PartitionSpec as P

SCREENING = 0.02
DAMPING = 0.8
LEAST_SWEEPS = 2
LANES = 128
HALF = LANES // 2
SUBLANES = 8
VMEM = pl.BlockSpec(memory_space=pltpu.VMEM)
HBM = pl.BlockSpec(memory_space=pltpu.HBM)
F32 = functools.partial(jax.ShapeDtypeStruct, dtype=jnp.float32)
SCRATCH = functools.partial(pltpu.VMEM, dtype=jnp.float32)


def in_hbm(array):
    return pltpu.with_memory_space_constraint(array, pltpu.HBM)


def diagonal(scale):
    return SCREENING + 4.0 * scale


def rows_of(value):
    return lax.broadcasted_iota(jnp.int32, value.shape, 0)


def lanes_of(tile):
    return lax.broadcasted_iota(jnp.int32, tile.shape, len(tile.shape) - 1)


def tiles(value):
    return [value[:, k * LANES:(k + 1) * LANES] for k in range(value.shape[1] // LANES)]


def row_before(value):
    return jnp.where(rows_of(value) == 0, 0.0, pltpu.roll(value, 1, 0))


def row_after(value):
    last = value.shape[0] - 1
    return jnp.where(rows_of(value) == last, 0.0, pltpu.roll(value, last, 0))


def norths(planes):
    return [row_before(planes[-1])] + list(planes[:-1])


def souths(planes):
    return list(planes[1:]) + [row_after(planes[0])]


def west_of(value):
    return pltpu.roll(value, 1, 1)


def east_of(value):
    return pltpu.roll(value, value.shape[1] - 1, 1)


def neighbours(groups, combine):
    cut = [[tiles(plane) for plane in planes] for planes in groups]
    count, wide = len(cut[0]), len(cut[0][0])
    lane = lanes_of(cut[0][0][0])
    known = {}

    def rolled(g, t, k, shift):
        place = (g, t, k % wide, shift)
        if place not in known:
            known[place] = pltpu.roll(cut[g][t][k % wide], shift, 1)
        return known[place]

    def west(g, t, k):
        if g:
            return cut[0][t][k]
        g = len(cut) - 1
        return jnp.where(lane == 0, rolled(g, t, k - 1, 1), rolled(g, t, k, 1))

    def east(g, t, k):
        if g + 1 < len(cut):
            return cut[1][t][k]
        return jnp.where(lane == LANES - 1, rolled(0, t, k + 1, LANES - 1), rolled(0, t, k, LANES - 1))

    out = []
    for g in range(len(cut)):
        group = []
        for t in range(count):
            done = []
            for k in range(wide):
                north = cut[g][t - 1][k] if t else row_before(cut[g][-1][k])
                south = cut[g][t + 1][k] if t + 1 < count else row_after(cut[g][0][k])
                done.append(combine(g, t, k, cut[g][t][k], (north + south) + (west(g, t, k) + east(g, t, k))))
            group.append(jnp.concatenate(done, 1))
        out.append(tuple(group))
    return tuple(out)


def sweep(groups, scaled, scale, inside=None):
    beside = DAMPING * scale / diagonal(scale)

    def combine(g, t, k, value, total):
        value = (1.0 - DAMPING) * value + (scaled(g, t, k) + beside * total)
        return value if inside is None else value * inside[t]

    return neighbours(groups, combine)


def residual(groups, scaled, scale):
    back = diagonal(scale) / DAMPING
    return neighbours(
        groups, lambda g, t, k, value, total: back * scaled(g, t, k) - diagonal(scale) * value + scale * total
    )


def span(k):
    return slice(k * LANES, (k + 1) * LANES)


def repeat(step, sweeps, level, fields, written, ready=lambda: None):
    for i in range(written):
        fields = step(i, fields)
    ready()
    return lax.fori_loop(LEAST_SWEEPS, sweeps[level], step, fields)


def load_planes(ref, start, count, height):
    def plane(first):
        rows = pl.ds(first, height, stride=count) if count > 1 else pl.ds(first, height)
        return jnp.concatenate([ref[k, rows, :] for k in range(ref.shape[0])], 1)

    return [plane(start + t) for t in range(count)]


def store_planes(ref, start, planes):
    count, height = len(planes), planes[0].shape[0]
    for t, plane in enumerate(planes):
        rows = pl.ds(start + t, height, stride=count) if count > 1 else pl.ds(start + t, height)
        for k, tile in enumerate(tiles(plane)):
            ref[k, rows, :] = tile


def places_of(shape, wanted):
    source = lax.broadcasted_iota(jnp.int32, shape, 0)
    target = lax.broadcasted_iota(jnp.int32, shape, 1)
    return wanted(source, target).astype(jnp.float32).astype(jnp.bfloat16)


def halo_quarter(fine):
    return jnp.where(fine < HALF, fine // 4, LANES - LANES // 4 + fine // 4)


def pairing():
    own = places_of((4 * LANES, 2 * LANES), lambda f, target: f // 4 + LANES * (f // 2 % 2) == target)
    halo = places_of((LANES, 2 * LANES), lambda f, target: halo_quarter(f) + LANES * (f // 2 % 2) == target)
    return own, halo


def merging():
    own = places_of((4 * LANES, 4 * LANES), lambda source, f: source == f // 4 + LANES * (f % 4))
    halo = places_of((4 * LANES, LANES), lambda source, f: source == halo_quarter(f) + LANES * (f % 4))
    return own, halo


def moved(value, places):
    high = value.astype(jnp.bfloat16)
    low = (value - high.astype(jnp.float32)).astype(jnp.bfloat16)
    dot = functools.partial(jnp.dot, preferred_element_type=jnp.float32)
    return dot(high, places) + dot(low, places)


def moved_blocks(own_blocks, halo_blocks, places):
    rows, count = halo_blocks[0].shape[0], len(own_blocks[0])
    packed = moved(jnp.concatenate([block for blocks in own_blocks for block in blocks], 0), places[0])
    edges = moved(jnp.concatenate(halo_blocks, 0), places[1])
    cut = lambda value, i: value[i * rows:(i + 1) * rows]
    return [[cut(packed, i * count + k) for k in range(count)] + [cut(edges, i)] for i in range(len(own_blocks))]


def pair_columns(fields, places):
    cols, width = fields[0].shape[1] - LANES, 4 * LANES
    own = [[f[:, k * width:(k + 1) * width] for k in range(cols // width)] for f in fields]
    moved_to = moved_blocks(own, [f[:, cols:] for f in fields], places)
    return [[[block[:, span(g)] for block in blocks] for g in range(2)] for blocks in moved_to]


def spread_rows(planes):
    return [
        half
        for value, north, south in zip(planes, norths(planes), souths(planes))
        for half in (0.75 * value + 0.25 * north, 0.75 * value + 0.25 * south)
    ]


def prolong(planes):
    planes = spread_rows(planes)
    return [
        [0.75 * value + 0.25 * west_of(value) for value in planes],
        [0.75 * value + 0.25 * east_of(value) for value in planes],
    ]


def prolong_merged(fields, places):
    own, halo = [], []
    for even, odd in fields:
        for e, o in zip(spread_rows(even), spread_rows(odd)):
            quarters = (
                0.75 * e + 0.25 * west_of(o),
                0.75 * e + 0.25 * o,
                0.75 * o + 0.25 * e,
                0.75 * o + 0.25 * east_of(e),
            )
            blocks = [jnp.concatenate(four, 1) for four in zip(*(tiles(q) for q in quarters))]
            own.append(blocks[:-1])
            halo.append(blocks[-1])
    planes = [jnp.concatenate(blocks, 1) for blocks in moved_blocks(own, halo, places)]
    count = len(planes) // len(fields)
    return [planes[i * count:(i + 1) * count] for i in range(len(fields))]


def window_of(rows, parts):
    return rows + (2 * SUBLANES if parts > 2 else SUBLANES if parts == 2 else 0)


def own_start(parts, place):
    return 0 if parts == 1 else pl.multiple_of(SUBLANES * place, SUBLANES) if parts == 2 else SUBLANES


def band_masks(window, parts, place, rows):
    if parts <= 2:
        return None
    count = window // SUBLANES
    first = place * rows - SUBLANES
    row = [first + t + count * lax.broadcasted_iota(jnp.int32, (SUBLANES, 1), 0) for t in range(count)]
    return [((r >= 0) & (r < parts * rows)).astype(jnp.float32) for r in row]


def eastward(own_last, halo):
    return jnp.where(lanes_of(halo) < HALF, halo, own_last)


def westward(own_first, halo):
    return jnp.where(lanes_of(halo) < HALF, own_first, halo)


def with_edges(parts, from_west, from_east):
    inner = lanes_of(from_west) < HALF
    first = parts[0] + jnp.where(inner, from_west, 0.0)
    last = parts[-2] + jnp.where(inner, 0.0, from_east)
    halo = parts[-1] + jnp.where(inner, from_east, from_west)
    return [first] + list(parts[1:-2]) + [last, halo]


COARSE_WIDTH, FINE_WIDTH, REACH = 16, 8, 4
TO_EAST, TO_WEST = -12, -4


def in_window(lane, start, width):
    start = start % LANES
    end = start + width
    return (lane >= start) & (lane < end) if end <= LANES else (lane >= start) | (lane < end - LANES)


def slots(heights, coarse_start):
    out, at = [], 0
    for which, rows in enumerate(heights):
        start, width = (-REACH, FINE_WIDTH) if which < 2 else (coarse_start, COARSE_WIDTH)
        for first in range(0, rows, SUBLANES):
            out.append((which, first, min(SUBLANES, rows - first), start, width, at))
            at += width
    assert at <= LANES
    return out


def bundle(fields, coarse_start):
    out = jnp.zeros((SUBLANES, LANES), jnp.float32)
    lane = lanes_of(out)
    for which, first, rows, start, width, at in slots([f.shape[0] for f in fields], coarse_start):
        piece = fields[which][first:first + rows]
        if rows < SUBLANES:
            piece = jnp.concatenate([piece, jnp.zeros((SUBLANES - rows, LANES), jnp.float32)], 0)
        out = jnp.where(in_window(lane, at, width), pltpu.roll(piece, (at - start) % LANES, 1), out)
    return out


def unbundle(tile, heights, coarse_start):
    lane = lanes_of(tile)
    pieces = [[] for _ in heights]
    for which, first, rows, start, width, at in slots(heights, coarse_start):
        piece = jnp.where(in_window(lane, start, width), pltpu.roll(tile, (start - at) % LANES, 1), 0.0)
        pieces[which].append(piece[:rows])
    return [jnp.concatenate(p, 0) if len(p) > 1 else p[0] for p in pieces]


COARSE_ROWS = 12
ACROSS = (SUBLANES, SUBLANES, COARSE_ROWS, COARSE_ROWS)


def border_rows(place):
    north, south = (pl.multiple_of(SUBLANES * (n - place), SUBLANES) for n in (1, 2))
    return pl.ds(north, SUBLANES), pl.ds(south, SUBLANES)


def border_value(place, ref):
    north, south = (ref[rows, :] for rows in border_rows(place))
    return jnp.where(rows_of(north) >= 4, north, south)


def border_right(place, ref):
    north, south = (ref[rows, :] for rows in border_rows(place))
    return jnp.where((place == 0) & (rows_of(north) != 4), north, pltpu.roll(south, 4, 0))


def add_border(place, value_ref, right_ref, value, right):
    row = rows_of(value)
    north, south = border_rows(place)
    value_ref[north, :] += jnp.where(row >= 4, value, 0.0)
    value_ref[south, :] += jnp.where(row < 4, value, 0.0)
    right_ref[north, :] += jnp.where((place == 1) & (row > 4), right, 0.0)
    right_ref[south, :] += jnp.where(row < jnp.where(place == 1, 1, 4), pltpu.roll(right, 4, 0), 0.0)


def half_tiles(lower, upper):
    return jnp.where(rows_of(lower) >= 4, lower, pltpu.roll(upper, 4, 0))


def pack(value, right, coarse):
    low = [tile for group in coarse for tile in group[:-1]]
    joined = [half_tiles(right[k], right[k + 1]) for k in range(0, len(right) - 1, 2)]
    joined += [jnp.concatenate([low[k][SUBLANES:], low[k + 1][SUBLANES:]], 0) for k in range(0, len(low), 2)]
    ends = bundle([value[-1], right[-1]] + [group[-1] for group in coarse], TO_WEST)
    return value[:-1] + [tile[:SUBLANES] for tile in low] + joined + [ends]


def packed_tiles(fine, coarse):
    return fine + coarse + (fine + coarse) // 2 + 1


def unpack(tile, fine, coarse):
    value = [tile(k) for k in range(fine)]
    right, low = [], []
    for k in range(fine // 2):
        both = tile(fine + coarse + k)
        right += [both, pltpu.roll(both, 4, 0)]
    for k in range(coarse // 2):
        both = tile(fine + coarse + fine // 2 + k)
        low += [jnp.concatenate([tile(fine + 2 * k + j), both[4 * j:4 * j + 4]], 0) for j in range(2)]
    ends = unbundle(tile(packed_tiles(fine, coarse) - 1), ACROSS, TO_WEST)
    fields = (value, right, low[:coarse // 2], low[coarse // 2:])
    return [field + [end] for field, end in zip(fields, ends)]


def down_kernel(parts, sweeps_hbm, target, grad_x, grad_y, labels, *refs):
    sent = 5 if parts == 2 else 0
    value_ref, right_ref, coarse_ref, merge_ref, merge_halo_ref = refs[:5]
    sent_refs = refs[5:5 + sent]
    sweeps, target_v, grad_x_v, grad_y_v, labels_v, v_ref, b_ref, scaled_ref, resid_ref, sems = refs[5 + sent:]
    chans, rows, cols = target.shape
    window = value_ref.shape[2]
    count = window // SUBLANES
    place = lax.axis_index("lat")
    start = own_start(parts, place)
    inside = band_masks(window, parts, place, rows)
    scale = 1.0

    first_copies = [
        pltpu.make_async_copy(labels, labels_v, sems.at[chans, 0]),
        pltpu.make_async_copy(sweeps_hbm, sweeps, sems.at[chans, 1]),
    ]
    for copy in first_copies:
        copy.start()
    copies = []
    for chan in range(chans):
        copies.append([
            pltpu.make_async_copy(target.at[chan], target_v.at[chan], sems.at[chan, 0]),
            pltpu.make_async_copy(grad_x.at[:, chan], grad_x_v.at[:, chan], sems.at[chan, 1]),
            pltpu.make_async_copy(grad_y.at[:, chan], grad_y_v.at[:, chan], sems.at[chan, 2]),
        ])
        for copy in copies[-1]:
            copy.start()
    if window > rows:
        v_ref[...] = jnp.zeros_like(v_ref)
        b_ref[...] = jnp.zeros_like(b_ref)
    places = pairing()
    merge_ref[...], merge_halo_ref[...] = merging()
    for copy in first_copies:
        copy.wait()

    def chosen(grad, chan):
        marks = labels_v[...]
        out = jnp.zeros((rows, cols), jnp.float32)
        for source in range(grad.shape[0]):
            out = jnp.where(marks == source, grad[source, chan], out)
        return out

    blank = jnp.zeros((rows, LANES), jnp.float32)
    fields = []
    for chan in range(chans):
        for copy in copies[chan]:
            copy.wait()
        own = jnp.concatenate([target_v[chan], blank], 1)
        sel_x = jnp.concatenate([chosen(grad_x_v, chan), blank], 1)
        sel_y = jnp.concatenate([chosen(grad_y_v, chan), blank], 1)
        right = SCREENING * own - ((sel_x - west_of(sel_x)) + (sel_y - row_before(sel_y)))
        below = pltpu.roll(sel_y[rows - SUBLANES:], 1, 0)
        below = jnp.where(rows_of(below) == 0, below, 0.0)
        for k, (v, b, s) in enumerate(zip(tiles(own), tiles(right), tiles(below))):
            v_ref[chan, k, pl.ds(start, rows), :] = v
            b_ref[chan, k, pl.ds(start, rows), :] = b
            if window > rows:
                b_ref[chan, k, pl.ds(start + rows, SUBLANES), :] = s
    for chan in range(chans):
        fields.append((tuple(load_planes(v_ref.at[chan], 0, count, SUBLANES)),))
        right = load_planes(b_ref.at[chan], 0, count, SUBLANES)
        if inside is not None:
            right = [b * mask for b, mask in zip(right, inside)]
        store_planes(right_ref.at[chan], 0, right)
        for t in range(count):
            scaled_ref[chan, t] = (DAMPING / diagonal(scale)) * right[t]

    def scaled(chan):
        return lambda g, t, k: scaled_ref[chan, t, :, span(k)]

    def step(_, fields):
        return tuple(sweep(field, scaled(chan), scale, inside) for chan, field in enumerate(fields))

    fields = repeat(step, sweeps, 0, tuple(fields), LEAST_SWEEPS)
    paired = []
    for chan, field in enumerate(fields):
        store_planes(value_ref.at[chan], 0, field[0])
        left = residual(field, scaled(chan), scale)[0]
        if inside is not None:
            left = [r * mask for r, mask in zip(left, inside)]
        store_planes(resid_ref.at[chan], 0, left)
    for chan in range(chans):
        north, south = load_planes(resid_ref.at[chan], 0, 2, window // 2)
        paired.append(north + south)
    coarse = pair_columns(paired, places)
    for chan in range(chans):
        low = [[0.25 * tile for tile in group] for group in coarse[chan]]
        coarse_ref[chan] = jnp.concatenate(low[0] + low[1], 1)
        if parts != 2:
            continue
        packed_ref, east_across, east_ref, west_across, west_ref = sent_refs
        wide = value_ref.shape[1]
        value = [value_ref[chan, k] for k in range(wide)]
        right = [right_ref[chan, k] for k in range(wide)]
        value_border = [border_value(place, value_ref.at[chan, k]) for k in range(wide)]
        right_border = [border_right(place, right_ref.at[chan, k]) for k in range(wide)]
        for k, tile in enumerate(pack(value_border, right_border, low)):
            packed_ref[chan, k] = tile
        for east, west, fields in (
            (east_ref, west_ref, (value, right, *low)),
            (east_across, west_across, (value_border, right_border, *low)),
        ):
            east[chan] = bundle([eastward(f[-2], f[-1]) for f in fields], TO_EAST)
            west[chan] = bundle([westward(f[0], f[-1]) for f in fields], TO_WEST)


def down(parts, sweeps, target, grad_x, grad_y, labels):
    chans, rows, cols = target.shape
    window = window_of(rows, parts)
    wide, quarter = cols // LANES + 1, cols // 4 // LANES + 1
    spare = SUBLANES if window > rows else 0
    outs = [F32((chans, wide, window, LANES))] * 2 + [F32((chans, window // 2, 2 * quarter * LANES))]
    outs += [jax.ShapeDtypeStruct((4 * LANES, n * LANES), jnp.bfloat16) for n in (4, 1)]
    if parts == 2:
        outs.append(F32((chans, packed_tiles(wide - 1, 2 * (quarter - 1)), SUBLANES, LANES)))
        outs += [F32((chans, SUBLANES, LANES))] * 4
    return pl.pallas_call(
        functools.partial(down_kernel, parts),
        in_specs=[HBM] * 5,
        out_specs=[VMEM] * len(outs),
        out_shape=outs,
        scratch_shapes=[
            pltpu.SMEM(sweeps.shape, jnp.int32),
            SCRATCH(target.shape),
            SCRATCH(grad_x.shape),
            SCRATCH(grad_y.shape),
            pltpu.VMEM(labels.shape, jnp.int32),
            SCRATCH((chans, wide, window + spare, LANES)),
            SCRATCH((chans, wide, window + spare, LANES)),
            SCRATCH((chans, window // SUBLANES, SUBLANES, wide * LANES)),
            SCRATCH((chans, wide, window, LANES)),
            pltpu.SemaphoreType.DMA((chans + 1, 3)),
        ],
        compiler_params=pltpu.CompilerParams(vmem_limit_bytes=32 * 2**20),
        name="down",
    )(*(in_hbm(a) for a in (sweeps, target, grad_x, grad_y, labels)))


def joined(place, own, other, height):
    gap = jnp.zeros((height - own.shape[0], own.shape[1]), jnp.float32)
    top, bottom = (lambda v: jnp.concatenate([v, gap], 0)), (lambda v: jnp.concatenate([gap, v], 0))
    return jnp.where(place == 0, top(own) + bottom(other), bottom(own) + top(other))


def up_kernel(parts, sweeps_hbm, value_ref, right_ref, coarse_ref, merge_ref, merge_halo_ref, *refs):
    received = 5 if parts == 2 else 0
    packed_ref, *edge_refs = refs[:received] or [None]
    out_hbm, sweeps, v0_ref, b0_ref, k0_ref, b1_ref, k1_ref, k2_ref, fix_ref, out_ref, sems = refs[received:]
    sweeps_copy = pltpu.make_async_copy(sweeps_hbm, sweeps, sems.at[0])
    sweeps_copy.start()
    chans, rows, cols = out_ref.shape
    wide, window = value_ref.shape[1:3]
    quarter = b1_ref.shape[2]
    full = parts * rows
    count0, count1 = window // SUBLANES, full // 2 // SUBLANES
    place = lax.axis_index("lat")
    inside = band_masks(window, parts, place, rows)
    own_heights = (window, window, window // 2, window // 2)

    def sides(chan, across):
        heights = ACROSS if across else own_heights
        from_west = unbundle(edge_refs[1 - across][chan], heights, TO_EAST)
        from_east = unbundle(edge_refs[3 - across][chan], heights, TO_WEST)
        return list(zip(from_west, from_east))

    for chan in range(chans):
        low = tiles(coarse_ref[chan])
        low = [low[:quarter], low[quarter:]]
        if parts == 2:
            here, there = sides(chan, 0), sides(chan, 1)
            other = unpack(lambda k: packed_ref[chan, k], wide - 1, 2 * (quarter - 1))
            value, right, *other_low = (with_edges(f, *s) for f, s in zip(other, there))
            low = [with_edges(f, *s) for f, s in zip(low, here[2:])]
            low = [[joined(place, a, b, full // 2) for a, b in zip(*both)] for both in zip(low, other_low)]
            for ref, own, side in ((v0_ref, value_ref, here[0]), (b0_ref, right_ref, here[1])):
                for k, tile in enumerate(with_edges([own[chan, k] for k in range(wide)], *side)):
                    ref[chan, k] = tile
            for k in range(wide):
                add_border(place, v0_ref.at[chan, k], b0_ref.at[chan, k], value[k], right[k])
        else:
            v0_ref[chan] = value_ref[chan]
            b0_ref[chan] = right_ref[chan]
        for g, group in enumerate(low):
            for k, tile in enumerate(group):
                b1_ref[chan, g, k] = tile

    def smoothed(fields, scaled_ref, level, written=LEAST_SWEEPS, ready=lambda: None):
        def step(_, fields):
            return tuple(
                sweep(field, lambda g, t, k, i=i: scaled_ref[i, g, t, :, span(k)], 0.25**level)
                for i, field in enumerate(fields)
            )

        fields = tuple(tuple(tuple(planes) for planes in field) for field in fields)
        return repeat(step, sweeps, level, fields, written, ready)

    def from_zero(rights, scaled_ref, level, ready=lambda: None):
        first = [[[(DAMPING / diagonal(0.25**level)) * b for b in planes] for planes in field] for field in rights]
        for i, field in enumerate(first):
            for g, planes in enumerate(field):
                for t, plane in enumerate(planes):
                    scaled_ref[i, g, t] = plane
        return smoothed(first, scaled_ref, level, LEAST_SWEEPS - 1, ready)

    right1 = [[load_planes(b1_ref.at[i, g], 0, count1, SUBLANES) for g in range(2)] for i in range(chans)]
    mid = from_zero(right1, k1_ref, 1, sweeps_copy.wait)
    right2 = []
    for i, field in enumerate(mid):
        even, odd = residual(field, lambda g, t, k, i=i: k1_ref[i, g, t, :, span(k)], 0.25)
        both = [a + b for a, b in zip(even, odd)]
        right2.append([[0.25 * (both[t] + both[t + 1]) for t in range(0, count1, 2)]])
    fix2 = from_zero(right2, k2_ref, 2)
    mid = [
        [[v + f for v, f in zip(planes, more)] for planes, more in zip(field, prolong(fix[0]))]
        for field, fix in zip(mid, fix2)
    ]
    mid = smoothed(mid, k1_ref, 1)
    spare = (fix_ref.shape[2] - full) // 2
    if spare:
        fix_ref[...] = jnp.zeros_like(fix_ref)
    for i, fix in enumerate(prolong_merged(mid, (merge_ref[...], merge_halo_ref[...]))):
        store_planes(fix_ref.at[i], spare, fix)
    shown = pl.multiple_of((SUBLANES if parts == 2 else rows) * place, SUBLANES)
    start = own_start(parts, place)
    fields = []
    for i in range(chans):
        planes = load_planes(v0_ref.at[i], 0, count0, SUBLANES)
        fix = load_planes(fix_ref.at[i], shown, count0, SUBLANES)
        fields.append((tuple(v + f for v, f in zip(planes, fix)),))
        for t, b in enumerate(load_planes(b0_ref.at[i], 0, count0, SUBLANES)):
            k0_ref[i, t] = (DAMPING / diagonal(1.0)) * b

    def step(_, fields):
        return tuple(
            sweep(field, lambda g, t, k, i=i: k0_ref[i, t, :, span(k)], 1.0, inside) for i, field in enumerate(fields)
        )

    fields = repeat(step, sweeps, 0, tuple(fields), LEAST_SWEEPS)
    out_copies = []
    for i, field in enumerate(fields):
        store_planes(v0_ref.at[i], 0, field[0])
        for k in range(cols // LANES):
            out_ref[i, :, k * LANES:(k + 1) * LANES] = v0_ref[i, k, pl.ds(start, rows), :]
        out_copies.append(pltpu.make_async_copy(out_ref.at[i], out_hbm.at[i], sems.at[1 + i]))
        out_copies[-1].start()
    for copy in out_copies:
        copy.wait()


def up(parts, shape, sweeps, value, right, coarse, *more):
    chans, rows, cols = shape
    wide, window = value.shape[1:3]
    full = parts * rows
    quarter = cols // 4 // LANES + 1
    count1, count2 = full // 2 // SUBLANES, full // 4 // SUBLANES
    spare = 2 * SUBLANES if parts > 2 else 0
    return pl.pallas_call(
        functools.partial(up_kernel, parts),
        in_specs=[HBM] + [VMEM] * (3 + len(more)),
        out_specs=HBM,
        out_shape=F32(shape),
        scratch_shapes=[
            pltpu.SMEM(sweeps.shape, jnp.int32),
            SCRATCH(value.shape),
            SCRATCH(value.shape),
            SCRATCH((chans, window // SUBLANES, SUBLANES, wide * LANES)),
            SCRATCH((chans, 2, quarter, full // 2, LANES)),
            SCRATCH((chans, 2, count1, SUBLANES, quarter * LANES)),
            SCRATCH((chans, 1, count2, SUBLANES, quarter * LANES)),
            SCRATCH((chans, wide, full + spare, LANES)),
            SCRATCH(shape),
            pltpu.SemaphoreType.DMA((1 + chans,)),
        ],
        compiler_params=pltpu.CompilerParams(vmem_limit_bytes=48 * 2**20),
        name="up",
    )(in_hbm(sweeps), value, right, coarse, *more)


def local(target, grad_x, grad_y, labels, sweeps):
    parts, around_globe = lax.axis_size("lat"), lax.axis_size("lon")
    value, right, coarse, merge, merge_halo, *sent = down(parts, sweeps, target, grad_x, grad_y, labels)
    eastward_pairs = [(i, (i + 1) % around_globe) for i in range(around_globe)]
    westward_pairs = [(j, i) for i, j in eastward_pairs]
    if parts < 2:
        raise NotImplementedError
    if parts == 2:
        def across(pairs):
            return [(2 * i + k, 2 * j + 1 - k) for i, j in pairs for k in range(2)]

        packed, east_across, east, west_across, west = sent
        packed = lax.ppermute(packed, "lat", [(0, 1), (1, 0)])
        across_west = lax.ppermute(east_across, ("lon", "lat"), across(eastward_pairs))
        from_west = lax.ppermute(east, "lon", eastward_pairs)
        across_east = lax.ppermute(west_across, ("lon", "lat"), across(westward_pairs))
        from_east = lax.ppermute(west, "lon", westward_pairs)
        received = (packed, across_west, from_west, across_east, from_east)
        return up(parts, target.shape, sweeps, value, right, coarse, merge, merge_halo, *received)

    chans, half_rows = coarse.shape[:2]
    coarse = coarse.reshape(chans, half_rows, -1, LANES).transpose(0, 2, 1, 3)

    def shared_lon(field):
        parts_of = [field[:, k] for k in range(field.shape[1])]
        from_west = lax.ppermute(eastward(parts_of[-2], parts_of[-1]), "lon", eastward_pairs)
        from_east = lax.ppermute(westward(parts_of[0], parts_of[-1]), "lon", westward_pairs)
        return jnp.stack(with_edges(parts_of, from_west, from_east), 1)

    value, right = shared_lon(value), shared_lon(right)
    halves = jnp.split(coarse, 2, axis=1)
    coarse = jnp.concatenate([shared_lon(f) for f in halves], 1)
    if parts > 2:
        rows = target.shape[1]
        spare = 2 * SUBLANES
        southward = [(i, i + 1) for i in range(parts - 1)]
        northward = [(i + 1, i) for i in range(parts - 1)]

        def shared_lat(field):
            north = lax.ppermute(field[:, :, rows:], "lat", southward)
            south = lax.ppermute(field[:, :, :spare], "lat", northward)
            zeros = jnp.zeros_like(south)
            return field + jnp.concatenate([north, zeros], 2) + jnp.concatenate([zeros, south], 2)

        value, right = shared_lat(value), shared_lat(right)
        every = lax.all_gather(coarse, "lat")
        step = rows // 2
        total = jnp.zeros((chans, coarse.shape[1], parts * step + SUBLANES, LANES), jnp.float32)
        for i in range(parts):
            total = total.at[:, :, i * step:i * step + step + SUBLANES].add(every[i])
        coarse = total[:, :, 4:-4]
    coarse = coarse.transpose(0, 2, 1, 3).reshape(chans, coarse.shape[2], -1)
    return up(parts, target.shape, sweeps, value, right, coarse, merge, merge_halo)


def solution(mesh):
    in_specs = (
        P(None, "lat", "lon"),
        P(None, None, "lat", "lon"),
        P(None, None, "lat", "lon"),
        P("lat", "lon"),
        P(),
    )
    out_specs = P(None, "lat", "lon")
    return jax.shard_map(local, mesh=mesh, in_specs=in_specs, out_specs=out_specs, check_vma=False)
```

time: 16.5 us -> 16.7 us (1.012)
  Pallas kernels: 6.24 us -> 6.47 us
where the time goes in v1:
time: 16.7 us; the launch traced here: 16.9 us
  starting transfers between devices  9.03 us (54%)
  Pallas kernels  6.47 us (39%)
  waiting for transfers between devices  1.41 us (8%)
    ppermute x1, starting transfers between devices, local(): lax.ppermute(west_across, ('lon', 'lat'), across(westward_pairs))  3.74 us
    pallas_call x1, Pallas kernels, up(): pl.pallas_call(functools.partial(up_kernel, parts), in_specs=[HBM] + [VME...  3.67 us
    ppermute x1, starting transfers between devices, local(): packed = lax.ppermute(packed, 'lat', [(0, 1), (1, 0)])  3.01 us
    pallas_call x1, Pallas kernels, down(): pl.pallas_call(functools.partial(down_kernel, parts), in_specs=[HBM] * 5,...  2.8 us
    ppermute x1, starting transfers between devices, local(): from_west = lax.ppermute(east, 'lon', eastward_pairs)  1.6 us
    ppermute x1, waiting for transfers between devices, local(): lax.ppermute(east_across, ('lon', 'lat'), across(eastward_pairs))  0.8 us
    ppermute x1, starting transfers between devices, local(): from_east = lax.ppermute(west, 'lon', westward_pairs)  0.68 us
    ppermute x1, waiting for transfers between devices, local(): from_east = lax.ppermute(west, 'lon', westward_pairs)  0.6 us
  transfers between devices with their start and end apart: 5, of which 2 were waited for; matrix products, arithmetic and copies ran while one was open for 0% of the time, Pallas kernels for 0%

profile of v1, /device:TPU:0, one launch (start us, length us, event | category | flops | bytes accessed | tf_op | source)
XLA Modules:
  0.0 16.9 jit_solution(16684117424930763337)
XLA Ops:
  0.0 2.8 %down.1 = (f32[3,9,24,128]{3,2,1,0:T(8,128)S(1)}, f32[3,9,24,128]{3,2,1,0:T(8,128)S(1)}, f32[3,12,768]{2,1,0:T(8,128)S(1)}, bf16[512,512]{1,0:T(8,128)(2,1)S(1)}...) custom-call(s32[3]{0:T(128)} %sweeps_hbm.3, ...), custom_call_target="tpu_custom_call" | custom-call | tf_op jit(solution)/shard_map/down/pallas_call | solution.py:475
  2.8 3.0 %collective-permute-start = (f32[3,19,8,128]{3,2,1,0:T(8,128)S(1)}, f32[3,19,8,128]{3,2,1,0:T(8,128)S(1)}, u32[]{:S(2)}, u32[]{:S(2)}) collective-permute-start(f32[3,19,8,128]{3,2,1,0:T(8,128)S(1)} %get-tuple-element.20), channel_id=1, source_target_pairs={{0,1},{1,0},{2,3},{3,2},{4,5},{5,4},{6,7},{7,6},{8,9},{9,8},{10,11... | collective-permute-start | bytes 700424 | tf_op jit(solution)/shard_map/ppermute | solution.py:649
  5.8 0.0 collective-permute-start.1
  5.8 1.6 %collective-permute-start.2 = (f32[3,8,128]{2,1,0:T(8,128)S(1)}, f32[3,8,128]{2,1,0:T(8,128)S(1)}, u32[]{:S(2)}, u32[]{:S(2)}) collective-permute-start(f32[3,8,128]{2,1,0:T(8,128)S(1)} %get-tuple-element.22), channel_id=1, source_target_pairs={{0,2},{2,4},{4,6},{6,8},{8,10},{10,12},{12,14},{14,16},{16,18},{18... | collective-permute-start | bytes 36872 | tf_op jit(solution)/shard_map/ppermute | solution.py:651
  7.4 3.7 %collective-permute-start.3 = (f32[3,8,128]{2,1,0:T(8,128)S(1)}, f32[3,8,128]{2,1,0:T(8,128)S(1)}, u32[]{:S(2)}, u32[]{:S(2)}) collective-permute-start(f32[3,8,128]{2,1,0:T(8,128)S(1)} %get-tuple-element.23), channel_id=1, source_target_pairs={{2,1},{3,0},{4,3},{5,2},{6,5},{7,4},{8,7},{9,6},{10,9},{11,8},{12,... | collective-permute-start | bytes 36872 | tf_op jit(solution)/shard_map/ppermute | solution.py:652
  11.2 0.7 %collective-permute-start.4 = (f32[3,8,128]{2,1,0:T(8,128)S(1)}, f32[3,8,128]{2,1,0:T(8,128)S(1)}, u32[]{:S(2)}, u32[]{:S(2)}) collective-permute-start(f32[3,8,128]{2,1,0:T(8,128)S(1)} %get-tuple-element.24), channel_id=1, source_target_pairs={{2,0},{4,2},{6,4},{8,6},{10,8},{12,10},{14,12},{16,14},{18,16},{20... | collective-permute-start | bytes 36872 | tf_op jit(solution)/shard_map/ppermute | solution.py:653
  11.8 0.8 %collective-permute-done.1.refs_1_ = f32[3,8,128]{2,1,0:T(8,128)S(1)} collective-permute-done((f32[3,8,128]{2,1,0:T(8,128)S(1)}, f32[3,8,128]{2,1,0:T(8,128)S(1)}, u32[]{:S(2)}, u32[]{:S(2)}) %collective-permute-start.1) | collective-permute-done | bytes 12320 | tf_op jit(solution)/shard_map/ppermute | solution.py:650
  12.6 0.0 collective-permute-done.2.refs_2_
  12.6 0.0 collective-permute-done.3.refs_3_
  12.6 0.6 %collective-permute-done.4.refs_4_ = f32[3,8,128]{2,1,0:T(8,128)S(1)} collective-permute-done((f32[3,8,128]{2,1,0:T(8,128)S(1)}, f32[3,8,128]{2,1,0:T(8,128)S(1)}, u32[]{:S(2)}, u32[]{:S(2)}) %collective-permute-start.4) | collective-permute-done | bytes 12320 | tf_op jit(solution)/shard_map/ppermute | solution.py:653
  13.2 0.0 collective-permute-done.refs_0_
  13.2 3.7 %up.1 = f32[3,16,1024]{2,1,0:T(8,128)} custom-call(s32[3]{0:T(128)} %sweeps_hbm.3, f32[3,9,24,128]{3,2,1,0:T(8,128)S(1)} %get-tuple-element.15.value_ref, f32[3,9,24,128]{3,2,1,0:T(8,128)S(1)} %get-tuple-element.16.right_ref, f32[3,12,768]{2,1,0:T(8,128)S(1)} %get-tuple-element.17.coarse_ref, bf16[512,512]{1,0:T(8,128)(2,1)S(1)} %get-tuple-element.18.merge_ref, ...), custom_call_target="tpu_custom_call" | custom-call | tf_op jit(solution)/shard_map/up/pallas_call | solution.py:615
Async XLA Ops:
  2.8 10.4 %collective-permute-start = (f32[3,19,8,128]{3,2,1,0:T(8,128)S(1)}, f32[3,19,8,128]{3,2,1,0:T(8,128)S(1)}, u32[]{:S(2)}, u32[]{:S(2)}) collective-permute-start(f32[3,19,8,128]{3,2,1,0:T(8,128)S(1)} %get-tuple-element.20), channel_id=1, source_target_pairs={{0,1},{1,0},{2,3},{3,2},{4,5},{5,4},{6,7},{7,6},{8,9},{9,8},{10,11... | collective-permute-start | bytes 700424 | tf_op jit(solution)/shard_map/ppermute | solution.py:649
  5.8 6.8 %collective-permute-start.1 = (f32[3,8,128]{2,1,0:T(8,128)S(1)}, f32[3,8,128]{2,1,0:T(8,128)S(1)}, u32[]{:S(2)}, u32[]{:S(2)}) collective-permute-start(f32[3,8,128]{2,1,0:T(8,128)S(1)} %get-tuple-element.21), channel_id=1, source_target_pairs={{0,3},{1,2},{2,5},{3,4},{4,7},{5,6},{6,9},{7,8},{8,11},{9,10},{10,... | collective-permute-start | bytes 36872 | tf_op jit(solution)/shard_map/ppermute | solution.py:650
  5.8 6.8 %collective-permute-start.2 = (f32[3,8,128]{2,1,0:T(8,128)S(1)}, f32[3,8,128]{2,1,0:T(8,128)S(1)}, u32[]{:S(2)}, u32[]{:S(2)}) collective-permute-start(f32[3,8,128]{2,1,0:T(8,128)S(1)} %get-tuple-element.22), channel_id=1, source_target_pairs={{0,2},{2,4},{4,6},{6,8},{8,10},{10,12},{12,14},{14,16},{16,18},{18... | collective-permute-start | bytes 36872 | tf_op jit(solution)/shard_map/ppermute | solution.py:651
  7.4 5.2 %collective-permute-start.3 = (f32[3,8,128]{2,1,0:T(8,128)S(1)}, f32[3,8,128]{2,1,0:T(8,128)S(1)}, u32[]{:S(2)}, u32[]{:S(2)}) collective-permute-start(f32[3,8,128]{2,1,0:T(8,128)S(1)} %get-tuple-element.23), channel_id=1, source_target_pairs={{2,1},{3,0},{4,3},{5,2},{6,5},{7,4},{8,7},{9,6},{10,9},{11,8},{12,... | collective-permute-start | bytes 36872 | tf_op jit(solution)/shard_map/ppermute | solution.py:652
  11.2 2.1 %collective-permute-start.4 = (f32[3,8,128]{2,1,0:T(8,128)S(1)}, f32[3,8,128]{2,1,0:T(8,128)S(1)}, u32[]{:S(2)}, u32[]{:S(2)}) collective-permute-start(f32[3,8,128]{2,1,0:T(8,128)S(1)} %get-tuple-element.24), channel_id=1, source_target_pairs={{2,0},{4,2},{6,4},{8,6},{10,8},{12,10},{14,12},{16,14},{18,16},{20... | collective-permute-start | bytes 36872 | tf_op jit(solution)/shard_map/ppermute | solution.py:653

commit v2 on v1

--- a/solution.py
+++ b/solution.py
@@ -9,7 +9,7 @@
 
 SCREENING = 0.02
 DAMPING = 0.8
-LEAST_SWEEPS = 2
+LEAST_SWEEPS, MOST_SWEEPS = 2, 4
 LANES = 128
 HALF = LANES // 2
 SUBLANES = 8
@@ -123,10 +123,18 @@
 
 
 def repeat(step, sweeps, level, fields, written, ready=lambda: None):
-    for i in range(written):
-        fields = step(i, fields)
+    def steps(count):
+        def run(fields):
+            for i in range(count):
+                fields = step(i, fields)
+            return fields
+
+        return run
+
+    fields = steps(written)(fields)
     ready()
-    return lax.fori_loop(LEAST_SWEEPS, sweeps[level], step, fields)
+    cases = [steps(more) for more in range(MOST_SWEEPS - LEAST_SWEEPS + 1)]
+    return lax.switch(sweeps[level] - LEAST_SWEEPS, cases, fields)
 
 
 def load_planes(ref, start, count, height):

time: 16.7 us -> 17.1 us (1.024); the launches traced: 16.9 us -> 16.9 us
  no operation moved by 1% of the time
where the time goes in v2:
time: 17.1 us; the launch traced here: 16.9 us
  starting transfers between devices  9.02 us (53%)
  Pallas kernels  6.46 us (38%)
  waiting for transfers between devices  1.41 us (8%)
    ppermute x1, starting transfers between devices, local(): lax.ppermute(west_across, ('lon', 'lat'), across(westward_pairs))  3.74 us
    pallas_call x1, Pallas kernels, up(): pl.pallas_call(functools.partial(up_kernel, parts), in_specs=[HBM] + [VME...  3.62 us
    ppermute x1, starting transfers between devices, local(): packed = lax.ppermute(packed, 'lat', [(0, 1), (1, 0)])  3 us
    pallas_call x1, Pallas kernels, down(): pl.pallas_call(functools.partial(down_kernel, parts), in_specs=[HBM] * 5,...  2.84 us
    ppermute x1, starting transfers between devices, local(): from_west = lax.ppermute(east, 'lon', eastward_pairs)  1.6 us
    ppermute x1, waiting for transfers between devices, local(): lax.ppermute(east_across, ('lon', 'lat'), across(eastward_pairs))  0.8 us
    ppermute x1, starting transfers between devices, local(): from_east = lax.ppermute(west, 'lon', westward_pairs)  0.68 us
    ppermute x1, waiting for transfers between devices, local(): from_east = lax.ppermute(west, 'lon', westward_pairs)  0.6 us
  transfers between devices with their start and end apart: 5, of which 2 were waited for; matrix products, arithmetic and copies ran while one was open for 0% of the time, Pallas kernels for 0%

profile of v2, /device:TPU:0, one launch (start us, length us, event | category | flops | bytes accessed | tf_op | source)
XLA Modules:
  0.0 16.9 jit_solution(5375875922600938640)
XLA Ops:
  0.0 2.8 %down.1 = (f32[3,9,24,128]{3,2,1,0:T(8,128)S(1)}, f32[3,9,24,128]{3,2,1,0:T(8,128)S(1)}, f32[3,12,768]{2,1,0:T(8,128)S(1)}, bf16[512,512]{1,0:T(8,128)(2,1)S(1)}...) custom-call(s32[3]{0:T(128)} %sweeps_hbm.3, ...), custom_call_target="tpu_custom_call" | custom-call | tf_op jit(solution)/shard_map/down/pallas_call | solution.py:483
  2.8 3.0 %collective-permute-start = (f32[3,19,8,128]{3,2,1,0:T(8,128)S(1)}, f32[3,19,8,128]{3,2,1,0:T(8,128)S(1)}, u32[]{:S(2)}, u32[]{:S(2)}) collective-permute-start(f32[3,19,8,128]{3,2,1,0:T(8,128)S(1)} %get-tuple-element.20), channel_id=1, source_target_pairs={{0,1},{1,0},{2,3},{3,2},{4,5},{5,4},{6,7},{7,6},{8,9},{9,8},{10,11... | collective-permute-start | bytes 700424 | tf_op jit(solution)/shard_map/ppermute | solution.py:657
  5.8 0.0 collective-permute-start.1
  5.9 1.6 %collective-permute-start.2 = (f32[3,8,128]{2,1,0:T(8,128)S(1)}, f32[3,8,128]{2,1,0:T(8,128)S(1)}, u32[]{:S(2)}, u32[]{:S(2)}) collective-permute-start(f32[3,8,128]{2,1,0:T(8,128)S(1)} %get-tuple-element.22), channel_id=1, source_target_pairs={{0,2},{2,4},{4,6},{6,8},{8,10},{10,12},{12,14},{14,16},{16,18},{18... | collective-permute-start | bytes 36872 | tf_op jit(solution)/shard_map/ppermute | solution.py:659
  7.5 3.7 %collective-permute-start.3 = (f32[3,8,128]{2,1,0:T(8,128)S(1)}, f32[3,8,128]{2,1,0:T(8,128)S(1)}, u32[]{:S(2)}, u32[]{:S(2)}) collective-permute-start(f32[3,8,128]{2,1,0:T(8,128)S(1)} %get-tuple-element.23), channel_id=1, source_target_pairs={{2,1},{3,0},{4,3},{5,2},{6,5},{7,4},{8,7},{9,6},{10,9},{11,8},{12,... | collective-permute-start | bytes 36872 | tf_op jit(solution)/shard_map/ppermute | solution.py:660
  11.2 0.7 %collective-permute-start.4 = (f32[3,8,128]{2,1,0:T(8,128)S(1)}, f32[3,8,128]{2,1,0:T(8,128)S(1)}, u32[]{:S(2)}, u32[]{:S(2)}) collective-permute-start(f32[3,8,128]{2,1,0:T(8,128)S(1)} %get-tuple-element.24), channel_id=1, source_target_pairs={{2,0},{4,2},{6,4},{8,6},{10,8},{12,10},{14,12},{16,14},{18,16},{20... | collective-permute-start | bytes 36872 | tf_op jit(solution)/shard_map/ppermute | solution.py:661
  11.9 0.8 %collective-permute-done.1.refs_1_ = f32[3,8,128]{2,1,0:T(8,128)S(1)} collective-permute-done((f32[3,8,128]{2,1,0:T(8,128)S(1)}, f32[3,8,128]{2,1,0:T(8,128)S(1)}, u32[]{:S(2)}, u32[]{:S(2)}) %collective-permute-start.1) | collective-permute-done | bytes 12320 | tf_op jit(solution)/shard_map/ppermute | solution.py:658
  12.7 0.0 collective-permute-done.2.refs_2_
  12.7 0.0 collective-permute-done.3.refs_3_
  12.7 0.6 %collective-permute-done.4.refs_4_ = f32[3,8,128]{2,1,0:T(8,128)S(1)} collective-permute-done((f32[3,8,128]{2,1,0:T(8,128)S(1)}, f32[3,8,128]{2,1,0:T(8,128)S(1)}, u32[]{:S(2)}, u32[]{:S(2)}) %collective-permute-start.4) | collective-permute-done | bytes 12320 | tf_op jit(solution)/shard_map/ppermute | solution.py:661
  13.3 0.0 collective-permute-done.refs_0_
  13.3 3.6 %up.1 = f32[3,16,1024]{2,1,0:T(8,128)} custom-call(s32[3]{0:T(128)} %sweeps_hbm.3, f32[3,9,24,128]{3,2,1,0:T(8,128)S(1)} %get-tuple-element.15.value_ref, f32[3,9,24,128]{3,2,1,0:T(8,128)S(1)} %get-tuple-element.16.right_ref, f32[3,12,768]{2,1,0:T(8,128)S(1)} %get-tuple-element.17.coarse_ref, bf16[512,512]{1,0:T(8,128)(2,1)S(1)} %get-tuple-element.18.merge_ref, ...), custom_call_target="tpu_custom_call" | custom-call | tf_op jit(solution)/shard_map/up/pallas_call | solution.py:623
Async XLA Ops:
  2.8 10.4 %collective-permute-start = (f32[3,19,8,128]{3,2,1,0:T(8,128)S(1)}, f32[3,19,8,128]{3,2,1,0:T(8,128)S(1)}, u32[]{:S(2)}, u32[]{:S(2)}) collective-permute-start(f32[3,19,8,128]{3,2,1,0:T(8,128)S(1)} %get-tuple-element.20), channel_id=1, source_target_pairs={{0,1},{1,0},{2,3},{3,2},{4,5},{5,4},{6,7},{7,6},{8,9},{9,8},{10,11... | collective-permute-start | bytes 700424 | tf_op jit(solution)/shard_map/ppermute | solution.py:657
  5.8 6.8 %collective-permute-start.1 = (f32[3,8,128]{2,1,0:T(8,128)S(1)}, f32[3,8,128]{2,1,0:T(8,128)S(1)}, u32[]{:S(2)}, u32[]{:S(2)}) collective-permute-start(f32[3,8,128]{2,1,0:T(8,128)S(1)} %get-tuple-element.21), channel_id=1, source_target_pairs={{0,3},{1,2},{2,5},{3,4},{4,7},{5,6},{6,9},{7,8},{8,11},{9,10},{10,... | collective-permute-start | bytes 36872 | tf_op jit(solution)/shard_map/ppermute | solution.py:658
  5.9 6.8 %collective-permute-start.2 = (f32[3,8,128]{2,1,0:T(8,128)S(1)}, f32[3,8,128]{2,1,0:T(8,128)S(1)}, u32[]{:S(2)}, u32[]{:S(2)}) collective-permute-start(f32[3,8,128]{2,1,0:T(8,128)S(1)} %get-tuple-element.22), channel_id=1, source_target_pairs={{0,2},{2,4},{4,6},{6,8},{8,10},{10,12},{12,14},{14,16},{16,18},{18... | collective-permute-start | bytes 36872 | tf_op jit(solution)/shard_map/ppermute | solution.py:659
  7.5 5.2 %collective-permute-start.3 = (f32[3,8,128]{2,1,0:T(8,128)S(1)}, f32[3,8,128]{2,1,0:T(8,128)S(1)}, u32[]{:S(2)}, u32[]{:S(2)}) collective-permute-start(f32[3,8,128]{2,1,0:T(8,128)S(1)} %get-tuple-element.23), channel_id=1, source_target_pairs={{2,1},{3,0},{4,3},{5,2},{6,5},{7,4},{8,7},{9,6},{10,9},{11,8},{12,... | collective-permute-start | bytes 36872 | tf_op jit(solution)/shard_map/ppermute | solution.py:660
  11.2 2.1 %collective-permute-start.4 = (f32[3,8,128]{2,1,0:T(8,128)S(1)}, f32[3,8,128]{2,1,0:T(8,128)S(1)}, u32[]{:S(2)}, u32[]{:S(2)}) collective-permute-start(f32[3,8,128]{2,1,0:T(8,128)S(1)} %get-tuple-element.24), channel_id=1, source_target_pairs={{2,0},{4,2},{6,4},{8,6},{10,8},{12,10},{14,12},{16,14},{18,16},{20... | collective-permute-start | bytes 36872 | tf_op jit(solution)/shard_map/ppermute | solution.py:661

commit v3 on v2

--- a/solution.py
+++ b/solution.py
@@ -363,12 +363,27 @@
     return [field + [end] for field, end in zip(fields, ends)]
 
 
+def merging_kernel(own_ref, halo_ref):
+    own_ref[...], halo_ref[...] = merging()
+
+
+def merging_places():
+    return pl.pallas_call(
+        merging_kernel,
+        out_specs=[VMEM] * 2,
+        out_shape=[jax.ShapeDtypeStruct((4 * LANES, n * LANES), jnp.bfloat16) for n in (4, 1)],
+        cost_estimate=pl.CostEstimate(flops=10**6, bytes_accessed=10**6, transcendentals=0),
+        name="merging",
+    )()
+
+
 def down_kernel(parts, sweeps_hbm, target, grad_x, grad_y, labels, *refs):
     sent = 5 if parts == 2 else 0
-    value_ref, right_ref, coarse_ref, merge_ref, merge_halo_ref = refs[:5]
-    sent_refs = refs[5:5 + sent]
-    sweeps, target_v, grad_x_v, grad_y_v, labels_v, v_ref, b_ref, scaled_ref, resid_ref, sems = refs[5 + sent:]
+    value_ref, right_ref, coarse_ref = refs[:3]
+    sent_refs = refs[3:3 + sent]
+    sweeps, target_v, grad_x_v, grad_y_v, labels_v, v_ref, b_ref, scaled_ref, resid_ref, sems = refs[3 + sent:]
     chans, rows, cols = target.shape
+    sources = grad_x.shape[0]
     window = value_ref.shape[2]
     count = window // SUBLANES
     place = lax.axis_index("lat")
@@ -384,18 +399,17 @@
         copy.start()
     copies = []
     for chan in range(chans):
-        copies.append([
-            pltpu.make_async_copy(target.at[chan], target_v.at[chan], sems.at[chan, 0]),
-            pltpu.make_async_copy(grad_x.at[:, chan], grad_x_v.at[:, chan], sems.at[chan, 1]),
-            pltpu.make_async_copy(grad_y.at[:, chan], grad_y_v.at[:, chan], sems.at[chan, 2]),
-        ])
+        copies.append([pltpu.make_async_copy(target.at[chan], target_v.at[chan], sems.at[chan, 0])])
+        for source in range(sources):
+            for i, (grad, here) in enumerate(((grad_x, grad_x_v), (grad_y, grad_y_v))):
+                sem = sems.at[chan, 1 + 2 * source + i]
+                copies[-1].append(pltpu.make_async_copy(grad.at[source, chan], here.at[source, chan], sem))
         for copy in copies[-1]:
             copy.start()
     if window > rows:
         v_ref[...] = jnp.zeros_like(v_ref)
         b_ref[...] = jnp.zeros_like(b_ref)
     places = pairing()
-    merge_ref[...], merge_halo_ref[...] = merging()
     for copy in first_copies:
         copy.wait()
 
@@ -476,7 +490,6 @@
     wide, quarter = cols // LANES + 1, cols // 4 // LANES + 1
     spare = SUBLANES if window > rows else 0
     outs = [F32((chans, wide, window, LANES))] * 2 + [F32((chans, window // 2, 2 * quarter * LANES))]
-    outs += [jax.ShapeDtypeStruct((4 * LANES, n * LANES), jnp.bfloat16) for n in (4, 1)]
     if parts == 2:
         outs.append(F32((chans, packed_tiles(wide - 1, 2 * (quarter - 1)), SUBLANES, LANES)))
         outs += [F32((chans, SUBLANES, LANES))] * 4
@@ -495,7 +508,7 @@
             SCRATCH((chans, wide, window + spare, LANES)),
             SCRATCH((chans, window // SUBLANES, SUBLANES, wide * LANES)),
             SCRATCH((chans, wide, window, LANES)),
-            pltpu.SemaphoreType.DMA((chans + 1, 3)),
+            pltpu.SemaphoreType.DMA((chans + 1, 1 + 2 * grad_x.shape[0])),
         ],
         compiler_params=pltpu.CompilerParams(vmem_limit_bytes=32 * 2**20),
         name="down",
@@ -644,7 +657,8 @@
 
 def local(target, grad_x, grad_y, labels, sweeps):
     parts, around_globe = lax.axis_size("lat"), lax.axis_size("lon")
-    value, right, coarse, merge, merge_halo, *sent = down(parts, sweeps, target, grad_x, grad_y, labels)
+    value, right, coarse, *sent = down(parts, sweeps, target, grad_x, grad_y, labels)
+    merge, merge_halo = merging_places()
     eastward_pairs = [(i, (i + 1) % around_globe) for i in range(around_globe)]
     westward_pairs = [(j, i) for i, j in eastward_pairs]
     if parts < 2:

time: 17.1 us -> 19.2 us (1.12); the launches traced: 16.9 us -> 19.3 us
  local copies, waits for them, and re-layouts: 0 us -> 1.95 us
  Pallas kernels: 6.46 us -> 7.84 us
  waiting for transfers between devices: 1.41 us -> 0.48 us
    unnamed x0 -> x4, local copies, waits for them, and re-layouts: none -> 1.95 us
    pallas_call x0 -> x1, Pallas kernels: none -> 0.93 us  [merging_places(): pl.pallas_call(merging_kernel, out_specs=[VMEM] * 2, out_shape=[jax.Shape...]
    ppermute x1, waiting for transfers between devices: 0.8 us -> 0.01 us  [local(): lax.ppermute(east_across, ('lon', 'lat'), across(eastward_pairs))]
    pallas_call x1, Pallas kernels: 3.62 us -> 3.89 us  [up(): pl.pallas_call(functools.partial(up_kernel, parts), in_specs=[HBM] + [VME...]
  transfers between devices with their start and end apart: 5 -> 5, of which waited for: 2 -> 1; matrix products, arithmetic and copies ran while one was open for 0% -> 0% of each run, Pallas kernels for 0% -> 5%
where the time goes in v3:
time: 19.2 us; the launch traced here: 19.3 us
  starting transfers between devices  9.02 us (47%)
  Pallas kernels  7.84 us (41%)
  local copies, waits for them, and re-layouts  1.95 us (10%)
  waiting for transfers between devices  0.48 us (2%)
    pallas_call x1, Pallas kernels, up(): pl.pallas_call(functools.partial(up_kernel, parts), in_specs=[HBM] + [VME...  3.89 us
    ppermute x1, starting transfers between devices, local(): lax.ppermute(west_across, ('lon', 'lat'), across(westward_pairs))  3.73 us
    pallas_call x1, Pallas kernels, down(): pl.pallas_call(functools.partial(down_kernel, parts), in_specs=[HBM] * 5,...  3.02 us
    ppermute x1, starting transfers between devices, local(): packed = lax.ppermute(packed, 'lat', [(0, 1), (1, 0)])  3 us
    unnamed x4, local copies, waits for them, and re-layouts  1.95 us
    ppermute x1, starting transfers between devices, local(): from_west = lax.ppermute(east, 'lon', eastward_pairs)  1.61 us
    pallas_call x1, Pallas kernels, merging_places(): pl.pallas_call(merging_kernel, out_specs=[VMEM] * 2, out_shape=[jax.Shape...  0.93 us
    ppermute x1, starting transfers between devices, local(): from_east = lax.ppermute(west, 'lon', westward_pairs)  0.68 us
  transfers between devices with their start and end apart: 5, of which 1 were waited for; matrix products, arithmetic and copies ran while one was open for 0% of the time, Pallas kernels for 5%

profile of v3, /device:TPU:0, one launch (start us, length us, event | category | flops | bytes accessed | tf_op | source)
XLA Modules:
  0.0 19.3 jit_solution(4100512350665848822)
XLA Ops:
  0.0 3.0 %down.1 = (f32[3,9,24,128]{3,2,1,0:T(8,128)S(1)}, f32[3,9,24,128]{3,2,1,0:T(8,128)S(1)}, f32[3,12,768]{2,1,0:T(8,128)S(1)}, f32[3,19,8,128]{3,2,1,0:T(8,128)S(1)...) custom-call(s32[3]{0:T(128)} %sweeps_hbm.3, ...), custom_call_target="tpu_custom_call" | custom-call | tf_op jit(solution)/shard_map/down/pallas_call | solution.py:496
  3.0 3.0 %collective-permute-start = (f32[3,19,8,128]{3,2,1,0:T(8,128)S(1)}, f32[3,19,8,128]{3,2,1,0:T(8,128)S(1)}, u32[]{:S(2)}, u32[]{:S(2)}) collective-permute-start(f32[3,19,8,128]{3,2,1,0:T(8,128)S(1)} %get-tuple-element.20), channel_id=1, source_target_pairs={{0,1},{1,0},{2,3},{3,2},{4,5},{5,4},{6,7},{7,6},{8,9},{9,8},{10,11... | collective-permute-start | bytes 700424 | tf_op jit(solution)/shard_map/ppermute | solution.py:671
  6.0 0.0 collective-permute-start.1
  6.0 1.6 %collective-permute-start.2 = (f32[3,8,128]{2,1,0:T(8,128)S(1)}, f32[3,8,128]{2,1,0:T(8,128)S(1)}, u32[]{:S(2)}, u32[]{:S(2)}) collective-permute-start(f32[3,8,128]{2,1,0:T(8,128)S(1)} %get-tuple-element.22), channel_id=1, source_target_pairs={{0,2},{2,4},{4,6},{6,8},{8,10},{10,12},{12,14},{14,16},{16,18},{18... | collective-permute-start | bytes 36872 | tf_op jit(solution)/shard_map/ppermute | solution.py:673
  7.6 3.7 %collective-permute-start.3 = (f32[3,8,128]{2,1,0:T(8,128)S(1)}, f32[3,8,128]{2,1,0:T(8,128)S(1)}, u32[]{:S(2)}, u32[]{:S(2)}) collective-permute-start(f32[3,8,128]{2,1,0:T(8,128)S(1)} %get-tuple-element.23), channel_id=1, source_target_pairs={{2,1},{3,0},{4,3},{5,2},{6,5},{7,4},{8,7},{9,6},{10,9},{11,8},{12,... | collective-permute-start | bytes 36872 | tf_op jit(solution)/shard_map/ppermute | solution.py:674
  11.4 0.7 %collective-permute-start.4 = (f32[3,8,128]{2,1,0:T(8,128)S(1)}, f32[3,8,128]{2,1,0:T(8,128)S(1)}, u32[]{:S(2)}, u32[]{:S(2)}) collective-permute-start(f32[3,8,128]{2,1,0:T(8,128)S(1)} %get-tuple-element.24), channel_id=1, source_target_pairs={{2,0},{4,2},{6,4},{8,6},{10,8},{12,10},{14,12},{16,14},{18,16},{20... | collective-permute-start | bytes 36872 | tf_op jit(solution)/shard_map/ppermute | solution.py:675
  12.1 0.9 %merging.1 = (bf16[512,512]{1,0:T(8,128)(2,1)}, bf16[512,128]{1,0:T(8,128)(2,1)}) custom-call(), custom_call_target="tpu_custom_call" | custom-call | flops 1000000 | bytes 1000000 | tf_op jit(solution)/shard_map/merging/pallas_call | solution.py:371
  13.0 0.0 collective-permute-done.1.refs_1_
  13.0 0.0 collective-permute-done.2.refs_2_
  13.0 0.0 collective-permute-done.3.refs_3_
  13.0 0.5 %collective-permute-done.4.refs_4_ = f32[3,8,128]{2,1,0:T(8,128)S(1)} collective-permute-done((f32[3,8,128]{2,1,0:T(8,128)S(1)}, f32[3,8,128]{2,1,0:T(8,128)S(1)}, u32[]{:S(2)}, u32[]{:S(2)}) %collective-permute-start.4) | collective-permute-done | bytes 12320 | tf_op jit(solution)/shard_map/ppermute | solution.py:675
  13.5 0.0 collective-permute-done.refs_0_
  13.5 0.0 copy-start
  13.5 1.0 %copy-done = bf16[512,512]{1,0:T(8,128)(2,1)S(1)} copy-done((bf16[512,512]{1,0:T(8,128)(2,1)S(1)}, bf16[512,512]{1,0:T(8,128)(2,1)}, u32[]{:S(2)}) %copy-start) | copy-done | bytes 524312
  14.5 0.0 copy-start.1
  14.5 0.9 %copy-done.1 = bf16[512,128]{1,0:T(8,128)(2,1)S(1)} copy-done((bf16[512,128]{1,0:T(8,128)(2,1)S(1)}, bf16[512,128]{1,0:T(8,128)(2,1)}, u32[]{:S(2)}) %copy-start.1) | copy-done | bytes 131096
  15.4 3.9 %up.1 = f32[3,16,1024]{2,1,0:T(8,128)} custom-call(s32[3]{0:T(128)} %sweeps_hbm.3, f32[3,9,24,128]{3,2,1,0:T(8,128)S(1)} %get-tuple-element.15.value_ref, f32[3,9,24,128]{3,2,1,0:T(8,128)S(1)} %get-tuple-element.16.right_ref, f32[3,12,768]{2,1,0:T(8,128)S(1)} %get-tuple-element.17.coarse_ref, bf16[512,512]{1,0:T(8,128)(2,1)S(1)} %copy-done, ...), custom_call_target="tpu_custom_call" | custom-call | tf_op jit(solution)/shard_map/up/pallas_call | solution.py:636
Async XLA Ops:
  3.0 10.4 %collective-permute-start = (f32[3,19,8,128]{3,2,1,0:T(8,128)S(1)}, f32[3,19,8,128]{3,2,1,0:T(8,128)S(1)}, u32[]{:S(2)}, u32[]{:S(2)}) collective-permute-start(f32[3,19,8,128]{3,2,1,0:T(8,128)S(1)} %get-tuple-element.20), channel_id=1, source_target_pairs={{0,1},{1,0},{2,3},{3,2},{4,5},{5,4},{6,7},{7,6},{8,9},{9,8},{10,11... | collective-permute-start | bytes 700424 | tf_op jit(solution)/shard_map/ppermute | solution.py:671
  6.0 7.0 %collective-permute-start.1 = (f32[3,8,128]{2,1,0:T(8,128)S(1)}, f32[3,8,128]{2,1,0:T(8,128)S(1)}, u32[]{:S(2)}, u32[]{:S(2)}) collective-permute-start(f32[3,8,128]{2,1,0:T(8,128)S(1)} %get-tuple-element.21), channel_id=1, source_target_pairs={{0,3},{1,2},{2,5},{3,4},{4,7},{5,6},{6,9},{7,8},{8,11},{9,10},{10,... | collective-permute-start | bytes 36872 | tf_op jit(solution)/shard_map/ppermute | solution.py:672
  6.0 7.0 %collective-permute-start.2 = (f32[3,8,128]{2,1,0:T(8,128)S(1)}, f32[3,8,128]{2,1,0:T(8,128)S(1)}, u32[]{:S(2)}, u32[]{:S(2)}) collective-permute-start(f32[3,8,128]{2,1,0:T(8,128)S(1)} %get-tuple-element.22), channel_id=1, source_target_pairs={{0,2},{2,4},{4,6},{6,8},{8,10},{10,12},{12,14},{14,16},{16,18},{18... | collective-permute-start | bytes 36872 | tf_op jit(solution)/shard_map/ppermute | solution.py:673
  7.6 5.3 %collective-permute-start.3 = (f32[3,8,128]{2,1,0:T(8,128)S(1)}, f32[3,8,128]{2,1,0:T(8,128)S(1)}, u32[]{:S(2)}, u32[]{:S(2)}) collective-permute-start(f32[3,8,128]{2,1,0:T(8,128)S(1)} %get-tuple-element.23), channel_id=1, source_target_pairs={{2,1},{3,0},{4,3},{5,2},{6,5},{7,4},{8,7},{9,6},{10,9},{11,8},{12,... | collective-permute-start | bytes 36872 | tf_op jit(solution)/shard_map/ppermute | solution.py:674
  11.4 2.1 %collective-permute-start.4 = (f32[3,8,128]{2,1,0:T(8,128)S(1)}, f32[3,8,128]{2,1,0:T(8,128)S(1)}, u32[]{:S(2)}, u32[]{:S(2)}) collective-permute-start(f32[3,8,128]{2,1,0:T(8,128)S(1)} %get-tuple-element.24), channel_id=1, source_target_pairs={{2,0},{4,2},{6,4},{8,6},{10,8},{12,10},{14,12},{16,14},{18,16},{20... | collective-permute-start | bytes 36872 | tf_op jit(solution)/shard_map/ppermute | solution.py:675
  13.5 1.0 %copy-start = (bf16[512,512]{1,0:T(8,128)(2,1)S(1)}, bf16[512,512]{1,0:T(8,128)(2,1)}, u32[]{:S(2)}) copy-start(bf16[512,512]{1,0:T(8,128)(2,1)} %get-tuple-element.18.merge_ref) | copy-start | bytes 1572868
  14.5 0.9 %copy-start.1 = (bf16[512,128]{1,0:T(8,128)(2,1)S(1)}, bf16[512,128]{1,0:T(8,128)(2,1)}, u32[]{:S(2)}) copy-start(bf16[512,128]{1,0:T(8,128)(2,1)} %get-tuple-element.19.merge_halo_ref) | copy-start | bytes 393220
